TPU v7x, 256 devices: a whole 4x4x8 slice. The times are simulated.
256 devices in a mesh: row: 8 (over x, core), col: 32 (over y, z).
Axes of the slice: x: 4, y: 4, z: 8, core: 2. Of those that a mesh axis runs over, the one named last changes fastest.
Arguments:
- source: bfloat16 [32768, 64], P(('row', 'col')), may hold values from -3 to 3
- target: bfloat16 [131072, 64], P(('col', 'row')), may hold values from -3 to 3
- log_a: float32 [32768], P('row'), may hold values from -1 to 1
- log_b: float32 [131072], P('col'), may hold values from -1 to 1
- start_potential: float32 [131072], P(('col', 'row')), may hold values from -8 to 300
Outputs:
- source_potential: float32 [32768], P(('row', 'col'))
- target_potential: float32 [131072], P(('col', 'row'))
All inputs are finite; a program needn't handle non-finite values.
Results may differ from a plain program's by a relative error of at most 0.0003.
Values may be sent and summed in bfloat16 or wider, within the bound.
No kernel may reach another device: no remote copies, remote signals or barrier semaphores. Data moves between devices by JAX's collectives and lax.ppermute only.
A program may use at most 64 MiB of HBM per device.

v0:
```python
import jax
import jax.numpy as jnp
from jax import lax
from jax.sharding import PartitionSpec as P


def merged(part, axis, combine):
    gathered = jax.tree.map(lambda a: lax.all_gather(a, axis), part)

    def take(source):
        return jax.tree.map(lambda a: lax.dynamic_index_in_dim(a, source, 0, False), gathered)

    return lax.fori_loop(
        1, lax.axis_size(axis), lambda source, state: combine(state, take(source)), take(0)
    )


def cost_tile(block, target, sq_y):
    dots = jnp.dot(block, target.T, preferred_element_type=jnp.float32)
    wide = block.astype(jnp.float32)
    sq_x = jnp.sum(wide * wide, axis=1)
    return 0.5 * sq_x[:, None] + 0.5 * sq_y[None, :] - dots


def combine(first, second):
    top = jnp.maximum(first[0], second[0])
    total = first[1] * jnp.exp(first[0] - top) + second[1] * jnp.exp(second[0] - top)
    return (top, total)


def per_device(source, target, log_a, log_b, start_potential):
    x_rows = lax.all_gather(source, "col", axis=0, tiled=True)
    y_cols = lax.all_gather(target, "row", axis=0, tiled=True)
    g_cols = lax.all_gather(start_potential, "row", axis=0, tiled=True)
    wide = y_cols.astype(jnp.float32)
    sq_y = jnp.sum(wide * wide, axis=1)
    src_rows = x_rows.shape[0]
    tgt_cols = y_cols.shape[0]
    rows = min(512, src_rows)
    count = src_rows // rows
    blocks = x_rows.reshape(count, rows, x_rows.shape[1])

    def row_pass(block):
        scores = g_cols[None, :] - cost_tile(block, y_cols, sq_y)
        peak = jnp.max(scores, axis=1)
        return (peak, jnp.sum(jnp.exp(scores - peak[:, None]), axis=1))

    row_max, row_sum = lax.map(row_pass, blocks)
    row_max = row_max.reshape(src_rows)
    row_sum = row_sum.reshape(src_rows)
    own_rows = src_rows // lax.axis_size("col")
    row_start = lax.axis_index("col") * own_rows
    top, total = merged((row_max, row_sum), "col", combine)
    f_rows = log_a - (top + jnp.log(total))
    f_own = lax.dynamic_slice_in_dim(f_rows, row_start, own_rows, 0)

    def col_pass(carry, inputs):
        block, fresh = inputs
        backward = fresh[:, None] - cost_tile(block, y_cols, sq_y)
        block_max = jnp.max(backward, axis=0)
        new_max = jnp.maximum(carry[0], block_max)
        new_sum = carry[1] * jnp.exp(carry[0] - new_max) + jnp.sum(
            jnp.exp(backward - new_max[None, :]), axis=0
        )
        return ((new_max, new_sum), None)

    start = (jnp.full((tgt_cols,), -1e30, jnp.float32), jnp.zeros((tgt_cols,), jnp.float32))
    (col_max, col_sum), unused = lax.scan(col_pass, start, (blocks, f_rows.reshape(count, rows)))
    own_cols = tgt_cols // lax.axis_size("row")
    col_start = lax.axis_index("row") * own_cols
    peak, total = merged((col_max, col_sum), "row", combine)
    g_all = log_b - (peak + jnp.log(total))
    g_own = lax.dynamic_slice_in_dim(g_all, col_start, own_cols, 0)
    return (f_own, g_own)


def solution(mesh):
    placed = (
        P(("row", "col"), None),
        P(("col", "row"), None),
        P("row"),
        P("col"),
        P(("col", "row")),
    )
    return jax.shard_map(
        per_device,
        mesh=mesh,
        in_specs=placed,
        out_specs=(P(("row", "col")), P(("col", "row"))),
        check_vma=False,
    )
```

profile of v0, /device:TPU:1, one launch (start us, length us, event | category | flops | bytes accessed | tf_op | source)
XLA Modules:
  0.0 363.5 jit_solution(249234910638166897)
XLA Ops:
  0.6 14.4 %all-gather.2 = f32[8,1,512]{2,1,0:T(1,128)S(1)} all-gather(f32[1,1,512]{2,1,0:T(1,128)} %bitcast.72), channel_id=1, replica_groups=mesh['row'=8,'col'=32] {'row'}, dimensions={0}, use_global_device_ids=true | all-gather | bytes 18432 | tf_op jit(solution)/shard_map/all_gather | solution.py:34
  15.1 40.6 %all_gather.28 = bf16[4096,64]{0,1:T(8,128)(2,1)S(1)} all-gather(bf16[128,64]{0,1:T(8,128)(2,1)} %param.13), channel_id=1, replica_groups=mesh['row'=8,'col'=32] {'col'}, dimensions={0}, use_global_device_ids=true | all-gather | bytes 540672 | tf_op jit(solution)/shard_map/all_gather | solution.py:32
  57.1 26.0 %all_gather.29 = bf16[4096,64]{1,0:T(8,128)(2,1)S(1)} all-gather(bf16[512,64]{1,0:T(8,128)(2,1)S(1)} %copy.10), channel_id=1, replica_groups=mesh['row'=8,'col'=32] {'row'}, dimensions={0}, use_global_device_ids=true | all-gather | bytes 589824 | tf_op jit(solution)/shard_map/all_gather | solution.py:33
  83.7 76.8 %while.59 = (s32[]{:T(128)}, f32[8,512]{1,0:T(8,128)S(1)}, f32[8,512]{1,0:T(8,128)S(1)}, f32[4096]{0:T(1024)S(1)}, bf16[8,512,64]{2,1,0:T(8,128)(2,1)S(1)}, /*in...) while((s32[]{:T(128)}, f32[8,512]{1,0:T(8,128)S(1)}, f32[8,512]{1,0:T(8,128)S(1)}, ...), condition=%wide.region_5.6_spmd, body=%wide.region_1.5_spmd.sunk | while | flops 287411200 | bytes 18145396 | solution.py:48
  83.9 4.7 %fusion.19 = (f32[512]{0:T(512)S(1)}, f32[512,4096]{1,0:T(8,128)}) fusion(f32[4096]{0:T(1024)S(1)} %broadcast_multiply_fusion.8, f32[512]{0:T(512)S(1)} %broadcast_multiply_fusion.9, f32[4096]{0:T(1024)S(1)} %get-tuple-element.629, bf16[4096,64]{1,0:T(8,128)(2,1)S(1)} %get-tuple-element.632, bf16[8,512,64]{2,1,0:T(8,128)(2,1)S(1)} %get-tuple-element.630, ...), kind=kOutput, calls=%fused_computation.2.clone.1 | convolution fusion | flops 276823552 | bytes 9605124 | tf_op jit(solution)/shard_map/while/body/eval_jaxpr/dot_general | solution.py:19
  88.6 4.6 %exponential_reduce_fusion.4 = f32[512]{0:T(512)S(1)} fusion(f32[512,4096]{1,0:T(8,128)} %get-tuple-element.580, f32[512]{0:T(512)S(1)} %get-tuple-element.579, f32[4096]{0:T(1024)S(1)} %broadcast_multiply_fusion.8, f32[512]{0:T(512)S(1)} %broadcast_multiply_fusion.9, f32[4096]{0:T(1024)S(1)} %get-tuple-element.629), kind=kLoop, calls=%fused_computation.clone.1 | loop fusion | flops 10485248 | bytes 8427520 | tf_op jit(solution)/shard_map/while/body/eval_jaxpr/reduce_sum | solution.py:46
  93.5 4.7 %fusion.19 = (f32[512]{0:T(512)S(1)}, f32[512,4096]{1,0:T(8,128)}) fusion(f32[4096]{0:T(1024)S(1)} %broadcast_multiply_fusion.8, f32[512]{0:T(512)S(1)} %broadcast_multiply_fusion.9, f32[4096]{0:T(1024)S(1)} %get-tuple-element.629, bf16[4096,64]{1,0:T(8,128)(2,1)S(1)} %get-tuple-element.632, bf16[8,512,64]{2,1,0:T(8,128)(2,1)S(1)} %get-tuple-element.630, ...), kind=kOutput, calls=%fused_computation.2.clone.1 | convolution fusion | flops 276823552 | bytes 9605124 | tf_op jit(solution)/shard_map/while/body/eval_jaxpr/dot_general | solution.py:19
  98.2 4.6 %exponential_reduce_fusion.4 = f32[512]{0:T(512)S(1)} fusion(f32[512,4096]{1,0:T(8,128)} %get-tuple-element.580, f32[512]{0:T(512)S(1)} %get-tuple-element.579, f32[4096]{0:T(1024)S(1)} %broadcast_multiply_fusion.8, f32[512]{0:T(512)S(1)} %broadcast_multiply_fusion.9, f32[4096]{0:T(1024)S(1)} %get-tuple-element.629), kind=kLoop, calls=%fused_computation.clone.1 | loop fusion | flops 10485248 | bytes 8427520 | tf_op jit(solution)/shard_map/while/body/eval_jaxpr/reduce_sum | solution.py:46
  103.1 4.7 %fusion.19 = (f32[512]{0:T(512)S(1)}, f32[512,4096]{1,0:T(8,128)}) fusion(f32[4096]{0:T(1024)S(1)} %broadcast_multiply_fusion.8, f32[512]{0:T(512)S(1)} %broadcast_multiply_fusion.9, f32[4096]{0:T(1024)S(1)} %get-tuple-element.629, bf16[4096,64]{1,0:T(8,128)(2,1)S(1)} %get-tuple-element.632, bf16[8,512,64]{2,1,0:T(8,128)(2,1)S(1)} %get-tuple-element.630, ...), kind=kOutput, calls=%fused_computation.2.clone.1 | convolution fusion | flops 276823552 | bytes 9605124 | tf_op jit(solution)/shard_map/while/body/eval_jaxpr/dot_general | solution.py:19
  107.8 4.6 %exponential_reduce_fusion.4 = f32[512]{0:T(512)S(1)} fusion(f32[512,4096]{1,0:T(8,128)} %get-tuple-element.580, f32[512]{0:T(512)S(1)} %get-tuple-element.579, f32[4096]{0:T(1024)S(1)} %broadcast_multiply_fusion.8, f32[512]{0:T(512)S(1)} %broadcast_multiply_fusion.9, f32[4096]{0:T(1024)S(1)} %get-tuple-element.629), kind=kLoop, calls=%fused_computation.clone.1 | loop fusion | flops 10485248 | bytes 8427520 | tf_op jit(solution)/shard_map/while/body/eval_jaxpr/reduce_sum | solution.py:46
  112.7 4.7 %fusion.19 = (f32[512]{0:T(512)S(1)}, f32[512,4096]{1,0:T(8,128)}) fusion(f32[4096]{0:T(1024)S(1)} %broadcast_multiply_fusion.8, f32[512]{0:T(512)S(1)} %broadcast_multiply_fusion.9, f32[4096]{0:T(1024)S(1)} %get-tuple-element.629, bf16[4096,64]{1,0:T(8,128)(2,1)S(1)} %get-tuple-element.632, bf16[8,512,64]{2,1,0:T(8,128)(2,1)S(1)} %get-tuple-element.630, ...), kind=kOutput, calls=%fused_computation.2.clone.1 | convolution fusion | flops 276823552 | bytes 9605124 | tf_op jit(solution)/shard_map/while/body/eval_jaxpr/dot_general | solution.py:19
  117.4 4.6 %exponential_reduce_fusion.4 = f32[512]{0:T(512)S(1)} fusion(f32[512,4096]{1,0:T(8,128)} %get-tuple-element.580, f32[512]{0:T(512)S(1)} %get-tuple-element.579, f32[4096]{0:T(1024)S(1)} %broadcast_multiply_fusion.8, f32[512]{0:T(512)S(1)} %broadcast_multiply_fusion.9, f32[4096]{0:T(1024)S(1)} %get-tuple-element.629), kind=kLoop, calls=%fused_computation.clone.1 | loop fusion | flops 10485248 | bytes 8427520 | tf_op jit(solution)/shard_map/while/body/eval_jaxpr/reduce_sum | solution.py:46
  122.3 4.7 %fusion.19 = (f32[512]{0:T(512)S(1)}, f32[512,4096]{1,0:T(8,128)}) fusion(f32[4096]{0:T(1024)S(1)} %broadcast_multiply_fusion.8, f32[512]{0:T(512)S(1)} %broadcast_multiply_fusion.9, f32[4096]{0:T(1024)S(1)} %get-tuple-element.629, bf16[4096,64]{1,0:T(8,128)(2,1)S(1)} %get-tuple-element.632, bf16[8,512,64]{2,1,0:T(8,128)(2,1)S(1)} %get-tuple-element.630, ...), kind=kOutput, calls=%fused_computation.2.clone.1 | convolution fusion | flops 276823552 | bytes 9605124 | tf_op jit(solution)/shard_map/while/body/eval_jaxpr/dot_general | solution.py:19
  127.0 4.6 %exponential_reduce_fusion.4 = f32[512]{0:T(512)S(1)} fusion(f32[512,4096]{1,0:T(8,128)} %get-tuple-element.580, f32[512]{0:T(512)S(1)} %get-tuple-element.579, f32[4096]{0:T(1024)S(1)} %broadcast_multiply_fusion.8, f32[512]{0:T(512)S(1)} %broadcast_multiply_fusion.9, f32[4096]{0:T(1024)S(1)} %get-tuple-element.629), kind=kLoop, calls=%fused_computation.clone.1 | loop fusion | flops 10485248 | bytes 8427520 | tf_op jit(solution)/shard_map/while/body/eval_jaxpr/reduce_sum | solution.py:46
  131.9 4.7 %fusion.19 = (f32[512]{0:T(512)S(1)}, f32[512,4096]{1,0:T(8,128)}) fusion(f32[4096]{0:T(1024)S(1)} %broadcast_multiply_fusion.8, f32[512]{0:T(512)S(1)} %broadcast_multiply_fusion.9, f32[4096]{0:T(1024)S(1)} %get-tuple-element.629, bf16[4096,64]{1,0:T(8,128)(2,1)S(1)} %get-tuple-element.632, bf16[8,512,64]{2,1,0:T(8,128)(2,1)S(1)} %get-tuple-element.630, ...), kind=kOutput, calls=%fused_computation.2.clone.1 | convolution fusion | flops 276823552 | bytes 9605124 | tf_op jit(solution)/shard_map/while/body/eval_jaxpr/dot_general | solution.py:19
  136.6 4.6 %exponential_reduce_fusion.4 = f32[512]{0:T(512)S(1)} fusion(f32[512,4096]{1,0:T(8,128)} %get-tuple-element.580, f32[512]{0:T(512)S(1)} %get-tuple-element.579, f32[4096]{0:T(1024)S(1)} %broadcast_multiply_fusion.8, f32[512]{0:T(512)S(1)} %broadcast_multiply_fusion.9, f32[4096]{0:T(1024)S(1)} %get-tuple-element.629), kind=kLoop, calls=%fused_computation.clone.1 | loop fusion | flops 10485248 | bytes 8427520 | tf_op jit(solution)/shard_map/while/body/eval_jaxpr/reduce_sum | solution.py:46
  141.5 4.7 %fusion.19 = (f32[512]{0:T(512)S(1)}, f32[512,4096]{1,0:T(8,128)}) fusion(f32[4096]{0:T(1024)S(1)} %broadcast_multiply_fusion.8, f32[512]{0:T(512)S(1)} %broadcast_multiply_fusion.9, f32[4096]{0:T(1024)S(1)} %get-tuple-element.629, bf16[4096,64]{1,0:T(8,128)(2,1)S(1)} %get-tuple-element.632, bf16[8,512,64]{2,1,0:T(8,128)(2,1)S(1)} %get-tuple-element.630, ...), kind=kOutput, calls=%fused_computation.2.clone.1 | convolution fusion | flops 276823552 | bytes 9605124 | tf_op jit(solution)/shard_map/while/body/eval_jaxpr/dot_general | solution.py:19
  146.2 4.6 %exponential_reduce_fusion.4 = f32[512]{0:T(512)S(1)} fusion(f32[512,4096]{1,0:T(8,128)} %get-tuple-element.580, f32[512]{0:T(512)S(1)} %get-tuple-element.579, f32[4096]{0:T(1024)S(1)} %broadcast_multiply_fusion.8, f32[512]{0:T(512)S(1)} %broadcast_multiply_fusion.9, f32[4096]{0:T(1024)S(1)} %get-tuple-element.629), kind=kLoop, calls=%fused_computation.clone.1 | loop fusion | flops 10485248 | bytes 8427520 | tf_op jit(solution)/shard_map/while/body/eval_jaxpr/reduce_sum | solution.py:46
  151.1 4.7 %fusion.19 = (f32[512]{0:T(512)S(1)}, f32[512,4096]{1,0:T(8,128)}) fusion(f32[4096]{0:T(1024)S(1)} %broadcast_multiply_fusion.8, f32[512]{0:T(512)S(1)} %broadcast_multiply_fusion.9, f32[4096]{0:T(1024)S(1)} %get-tuple-element.629, bf16[4096,64]{1,0:T(8,128)(2,1)S(1)} %get-tuple-element.632, bf16[8,512,64]{2,1,0:T(8,128)(2,1)S(1)} %get-tuple-element.630, ...), kind=kOutput, calls=%fused_computation.2.clone.1 | convolution fusion | flops 276823552 | bytes 9605124 | tf_op jit(solution)/shard_map/while/body/eval_jaxpr/dot_general | solution.py:19
  160.5 36.3 %all-gather.3 = f32[32,1,4096]{2,1,0:T(1,128)S(1)} all-gather(f32[1,1,4096]{2,1,0:T(1,128)S(1)} %reshape.41), channel_id=1, replica_groups=mesh['row'=8,'col'=32] {'col'}, dimensions={0}, use_global_device_ids=true | all-gather | bytes 540672 | tf_op jit(solution)/shard_map/all_gather | solution.py:8
  196.9 35.6 %all-gather.4 = f32[32,1,4096]{2,1,0:T(1,128)S(1)} all-gather(f32[1,1,4096]{2,1,0:T(1,128)S(1)} %reshape.43), channel_id=1, replica_groups=mesh['row'=8,'col'=32] {'col'}, dimensions={0}, use_global_device_ids=true | all-gather | bytes 540672 | tf_op jit(solution)/shard_map/all_gather | solution.py:8
  236.4 75.9 %while.62 = (s32[]{:T(128)}, f32[4096]{0:T(1024)S(1)}, f32[4096]{0:T(1024)S(1)}, f32[8,512]{1,0:T(8,128)S(1)}, bf16[8,512,64]{2,1,0:T(8,128)(2,1)S(1)}, /*index=...) while((s32[]{:T(128)}, f32[4096]{0:T(1024)S(1)}, f32[4096]{0:T(1024)S(1)}, ...), condition=%wide.region_12.13_spmd.clone, body=%wide.region_8.12_spmd.clone.sunk | while | flops 287432704 | bytes 18319484 | solution.py:68
  236.6 4.6 %fusion.21 = (f32[4096]{0:T(1024)S(1)}, f32[512,4096]{1,0:T(8,128)}) fusion(f32[4096]{0:T(1024)S(1)} %broadcast_multiply_fusion.10, f32[512]{0:T(512)S(1)} %broadcast_multiply_fusion.11, f32[512]{0:T(512)S(1)} %bitcast.70, bf16[4096,64]{1,0:T(8,128)(2,1)S(1)} %get-tuple-element.683, bf16[8,512,64]{2,1,0:T(8,128)(2,1)S(1)} %get-tuple-element.681, ...), kind=kOutput, calls=%fused_computation.18.clone.1 | convolution fusion | flops 276819968 | bytes 9605124 | tf_op jit(solution)/shard_map/while/body/eval_jaxpr/dot_general | solution.py:19
  246.1 4.6 %fusion.21 = (f32[4096]{0:T(1024)S(1)}, f32[512,4096]{1,0:T(8,128)}) fusion(f32[4096]{0:T(1024)S(1)} %broadcast_multiply_fusion.10, f32[512]{0:T(512)S(1)} %broadcast_multiply_fusion.11, f32[512]{0:T(512)S(1)} %bitcast.70, bf16[4096,64]{1,0:T(8,128)(2,1)S(1)} %get-tuple-element.683, bf16[8,512,64]{2,1,0:T(8,128)(2,1)S(1)} %get-tuple-element.681, ...), kind=kOutput, calls=%fused_computation.18.clone.1 | convolution fusion | flops 276819968 | bytes 9605124 | tf_op jit(solution)/shard_map/while/body/eval_jaxpr/dot_general | solution.py:19
  255.5 4.6 %fusion.21 = (f32[4096]{0:T(1024)S(1)}, f32[512,4096]{1,0:T(8,128)}) fusion(f32[4096]{0:T(1024)S(1)} %broadcast_multiply_fusion.10, f32[512]{0:T(512)S(1)} %broadcast_multiply_fusion.11, f32[512]{0:T(512)S(1)} %bitcast.70, bf16[4096,64]{1,0:T(8,128)(2,1)S(1)} %get-tuple-element.683, bf16[8,512,64]{2,1,0:T(8,128)(2,1)S(1)} %get-tuple-element.681, ...), kind=kOutput, calls=%fused_computation.18.clone.1 | convolution fusion | flops 276819968 | bytes 9605124 | tf_op jit(solution)/shard_map/while/body/eval_jaxpr/dot_general | solution.py:19
  265.0 4.6 %fusion.21 = (f32[4096]{0:T(1024)S(1)}, f32[512,4096]{1,0:T(8,128)}) fusion(f32[4096]{0:T(1024)S(1)} %broadcast_multiply_fusion.10, f32[512]{0:T(512)S(1)} %broadcast_multiply_fusion.11, f32[512]{0:T(512)S(1)} %bitcast.70, bf16[4096,64]{1,0:T(8,128)(2,1)S(1)} %get-tuple-element.683, bf16[8,512,64]{2,1,0:T(8,128)(2,1)S(1)} %get-tuple-element.681, ...), kind=kOutput, calls=%fused_computation.18.clone.1 | convolution fusion | flops 276819968 | bytes 9605124 | tf_op jit(solution)/shard_map/while/body/eval_jaxpr/dot_general | solution.py:19
  274.5 4.6 %fusion.21 = (f32[4096]{0:T(1024)S(1)}, f32[512,4096]{1,0:T(8,128)}) fusion(f32[4096]{0:T(1024)S(1)} %broadcast_multiply_fusion.10, f32[512]{0:T(512)S(1)} %broadcast_multiply_fusion.11, f32[512]{0:T(512)S(1)} %bitcast.70, bf16[4096,64]{1,0:T(8,128)(2,1)S(1)} %get-tuple-element.683, bf16[8,512,64]{2,1,0:T(8,128)(2,1)S(1)} %get-tuple-element.681, ...), kind=kOutput, calls=%fused_computation.18.clone.1 | convolution fusion | flops 276819968 | bytes 9605124 | tf_op jit(solution)/shard_map/while/body/eval_jaxpr/dot_general | solution.py:19
  284.0 4.6 %fusion.21 = (f32[4096]{0:T(1024)S(1)}, f32[512,4096]{1,0:T(8,128)}) fusion(f32[4096]{0:T(1024)S(1)} %broadcast_multiply_fusion.10, f32[512]{0:T(512)S(1)} %broadcast_multiply_fusion.11, f32[512]{0:T(512)S(1)} %bitcast.70, bf16[4096,64]{1,0:T(8,128)(2,1)S(1)} %get-tuple-element.683, bf16[8,512,64]{2,1,0:T(8,128)(2,1)S(1)} %get-tuple-element.681, ...), kind=kOutput, calls=%fused_computation.18.clone.1 | convolution fusion | flops 276819968 | bytes 9605124 | tf_op jit(solution)/shard_map/while/body/eval_jaxpr/dot_general | solution.py:19
  293.5 4.6 %fusion.21 = (f32[4096]{0:T(1024)S(1)}, f32[512,4096]{1,0:T(8,128)}) fusion(f32[4096]{0:T(1024)S(1)} %broadcast_multiply_fusion.10, f32[512]{0:T(512)S(1)} %broadcast_multiply_fusion.11, f32[512]{0:T(512)S(1)} %bitcast.70, bf16[4096,64]{1,0:T(8,128)(2,1)S(1)} %get-tuple-element.683, bf16[8,512,64]{2,1,0:T(8,128)(2,1)S(1)} %get-tuple-element.681, ...), kind=kOutput, calls=%fused_computation.18.clone.1 | convolution fusion | flops 276819968 | bytes 9605124 | tf_op jit(solution)/shard_map/while/body/eval_jaxpr/dot_general | solution.py:19
  303.0 4.6 %fusion.21 = (f32[4096]{0:T(1024)S(1)}, f32[512,4096]{1,0:T(8,128)}) fusion(f32[4096]{0:T(1024)S(1)} %broadcast_multiply_fusion.10, f32[512]{0:T(512)S(1)} %broadcast_multiply_fusion.11, f32[512]{0:T(512)S(1)} %bitcast.70, bf16[4096,64]{1,0:T(8,128)(2,1)S(1)} %get-tuple-element.683, bf16[8,512,64]{2,1,0:T(8,128)(2,1)S(1)} %get-tuple-element.681, ...), kind=kOutput, calls=%fused_computation.18.clone.1 | convolution fusion | flops 276819968 | bytes 9605124 | tf_op jit(solution)/shard_map/while/body/eval_jaxpr/dot_general | solution.py:19
  312.3 36.5 %all-gather = f32[32768]{0:T(1024)S(1)} all-gather(f32[4096]{0:T(1024)S(1)} %get-tuple-element.348), channel_id=2, replica_groups=mesh['row'=8,'col'=32] {'row'}, dimensions={0}, use_global_device_ids=true | all-gather | bytes 147456 | tf_op jit(solution)/shard_map/all_gather | solution.py:8
  348.7 12.7 %all-gather.1 = f32[32768]{0:T(1024)S(1)} all-gather(f32[4096]{0:T(1024)S(1)} %get-tuple-element.349), channel_id=3, replica_groups=mesh['row'=8,'col'=32] {'row'}, dimensions={0}, use_global_device_ids=true | all-gather | bytes 147456 | tf_op jit(solution)/shard_map/all_gather | solution.py:8
  (206 shorter events, 54.8 us)
Async XLA Ops:
  83.7 152.1 %copy-start = (f32[4096]{0:T(1024)S(1)}, f32[4096]{0:T(1024)}, u32[]{:S(2)}) copy-start(f32[4096]{0:T(1024)} %param.15) | copy-start | bytes 49156
where the time goes:
time: 364 us; the launch traced here: 363 us
  blocking collectives  202 us (55%)
  other arithmetic  79.1 us (22%)
  matrix products  74.6 us (20%)
  local copies, waits for them, and re-layouts  4.76 us (1%)
    all_gather x4, blocking collectives, merged(): gathered = jax.tree.map(lambda a: lax.all_gather(a, axis), part)  121 us
    dot_general x16, matrix products, cost_tile(): dots = jnp.dot(block, target.T, preferred_element_type=jnp.float32)  74.6 us
    all_gather x1, blocking collectives, per_device(): x_rows = lax.all_gather(source, 'col', axis=0, tiled=True)  40.6 us
    reduce_sum x8, other arithmetic, row_pass(): return (peak, jnp.sum(jnp.exp(scores - peak[:, None]), axis=1))  36.9 us
    reduce_sum x8, other arithmetic, col_pass(): jnp.sum(jnp.exp(backward - new_max[None, :]), axis=0)  36.7 us
    all_gather x1, blocking collectives, per_device(): y_cols = lax.all_gather(target, 'row', axis=0, tiled=True)  26 us
    all_gather x1, blocking collectives, per_device(): g_cols = lax.all_gather(start_potential, 'row', axis=0, tiled=True)  14.4 us

commit v1 on v0

v1 whole, which is shorter than its diff:
```python
import functools

import jax
import jax.numpy as jnp
from jax import lax
from jax.experimental import pallas as pl
from jax.experimental.pallas import tpu as pltpu
from jax.sharding import PartitionSpec as P

F32 = jnp.float32
BF16 = jnp.bfloat16
LANES = 128
PACKED = 256
PIECE = PACKED + 16
LOW, HIGH = 1e-24, 1e36


def params(mib=36):
    return pltpu.CompilerParams(vmem_limit_bytes=mib * 2**20)


def lanes_to_rows(values):
    return jnp.broadcast_to(values, (LANES, LANES)).T


def times(left, right):
    return lax.dot_general(left, right, (((1,), (1,)), ((), ())), preferred_element_type=F32)


def wide(rows, columns):
    return jnp.concatenate([rows] * (columns // LANES), axis=1)


def fold(values, combine):
    rows, columns = values.shape
    return combine(values.reshape(rows // 8, 8, columns), axis=0)


def prepare_kernel(x_ref, y_ref, g_ref, xs_ref, ys_ref, sqx_ref, sqy_ref, part_ref):
    half = x_ref.shape[0] // 2
    x = x_ref[...]
    packed = jnp.concatenate([x[:half], x[half:]], axis=1)
    for peer in range(xs_ref.shape[0]):
        xs_ref[peer] = packed
    xt = x.astype(F32).T
    sqx_ref[...] = jnp.sum(xt * xt, axis=0, keepdims=True)
    y = y_ref[...]
    ys_ref[pl.ds(0, PACKED), :] = jnp.concatenate([y[:PACKED], y[PACKED:]], axis=1)
    yt = y.astype(F32).T
    sqy = jnp.sum(yt * yt, axis=0, keepdims=True)
    part_ref[...] = jnp.zeros_like(part_ref)
    for k in range(4):
        own = sqy[:, k * LANES : (k + 1) * LANES]
        sqy_ref[pl.ds(k, 1), :] = own
        rest = g_ref[pl.ds(k, 1), :] - 0.5 * own
        for level in range(3):
            part = rest.astype(BF16).astype(F32)
            part_ref[pl.ds(4 * level + k, 1), :] = part
            rest = rest - part
    ys_ref[pl.ds(PACKED, 16), :] = part_ref[...].astype(BF16)


def prepare(source, target, g, peers):
    return pl.pallas_call(
        prepare_kernel,
        out_shape=(
            jax.ShapeDtypeStruct((peers, 64, LANES), BF16),
            jax.ShapeDtypeStruct((PIECE, LANES), BF16),
            jax.ShapeDtypeStruct((1, LANES), F32),
            jax.ShapeDtypeStruct((4, LANES), F32),
        ),
        scratch_shapes=[pltpu.VMEM((16, LANES), F32)],
        name="prepare",
        compiler_params=params(),
    )(source, target, g.reshape(4, LANES))


def pieces_of(refs):
    return [ref.at[k] for ref in refs for k in range(ref.shape[0])]


def spread(xs_ref, x1, x2):
    zeros = jnp.zeros((64, 64), BF16)
    for q in range(xs_ref.shape[0]):
        both = xs_ref[q]
        top, low = both[:, :64], both[:, 64:]
        x1[pl.ds(q * 128, 64), :] = jnp.concatenate([top, zeros], axis=1)
        x1[pl.ds(q * 128 + 64, 64), :] = jnp.concatenate([low, zeros], axis=1)
        x2[pl.ds(q * 128, 64), :] = jnp.concatenate([zeros, top], axis=1)
        x2[pl.ds(q * 128 + 64, 64), :] = jnp.concatenate([zeros, low], axis=1)


def row_kernel(xs_ref, *refs, groups):
    y_refs, (lp_ref, x1, x2, h1, h2) = refs[:groups], refs[groups:]
    ys = pieces_of(y_refs)
    rows = x1.shape[0]
    tile = 1024
    spread(xs_ref, x1, x2)
    terms = []
    for y in ys:
        parts = y[pl.ds(PACKED, 16), :].astype(F32)
        terms.append(parts[0:4] + parts[4:8] + parts[8:12])
    shift = jnp.max(functools.reduce(jnp.maximum, terms))
    for p, term in enumerate(terms):
        term = term - shift
        for k in range(2):
            at = pl.ds(p * PACKED + k * LANES, LANES)
            h1[at, :] = lanes_to_rows(term[k : k + 1])
            h2[at, :] = lanes_to_rows(term[k + 2 : k + 3])

    def scores(p, x, h, n, columns):
        z = times(ys[p][pl.ds(0, PACKED), :], x[pl.ds(n * columns, columns), :])
        return z + wide(h[pl.ds(p * PACKED, PACKED), :], columns)

    def total(n, seen):
        acc = jnp.zeros((8, tile), F32)
        for p in range(len(ys)):
            for x, h in ((x1, h1), (x2, h2)):
                acc += fold(jnp.exp(scores(p, x, h, n, tile)), jnp.sum)
        total = jnp.sum(acc, axis=0, keepdims=True)
        lp = shift + jnp.log(total)
        for k in range(tile // LANES):
            lp_ref[pl.ds(n * (tile // LANES) + k, 1), :] = lp[:, k * LANES : (k + 1) * LANES]
        return jnp.minimum(seen[0], jnp.min(total)), jnp.maximum(seen[1], jnp.max(total))

    least, most = lax.fori_loop(0, rows // tile, total, (jnp.float32(1.0), jnp.float32(1.0)))

    @pl.when(jnp.logical_not((least > LOW) & (most < HIGH)))
    def _():
        def exact(n, carry):
            peak = jnp.full((8, LANES), -1e30, F32)
            for p in range(len(ys)):
                for x, h in ((x1, h1), (x2, h2)):
                    peak = jnp.maximum(peak, fold(scores(p, x, h, n, LANES), jnp.max))
            peak = jnp.max(peak, axis=0, keepdims=True)
            acc = jnp.zeros((8, LANES), F32)
            for p in range(len(ys)):
                for x, h in ((x1, h1), (x2, h2)):
                    acc += fold(jnp.exp(scores(p, x, h, n, LANES) - peak), jnp.sum)
            total = jnp.sum(acc, axis=0, keepdims=True)
            lp_ref[pl.ds(n, 1), :] = shift + peak + jnp.log(total)
            return carry

        lax.fori_loop(0, rows // LANES, exact, 0)


def row_pass(xs, ys):
    peers = xs.shape[0]
    rows = peers * 128
    packed = sum(y.shape[0] for y in ys) * PACKED
    return pl.pallas_call(
        functools.partial(row_kernel, groups=len(ys)),
        out_shape=jax.ShapeDtypeStruct((peers, LANES), F32),
        scratch_shapes=[
            pltpu.VMEM((rows, LANES), BF16),
            pltpu.VMEM((rows, LANES), BF16),
            pltpu.VMEM((packed, LANES), F32),
            pltpu.VMEM((packed, LANES), F32),
        ],
        name="row_pass",
        compiler_params=params(),
        cost_estimate=pl.CostEstimate(
            flops=4 * rows * packed * 128, bytes_accessed=4 * 2**20, transcendentals=2 * rows * packed
        ),
    )(xs, *ys)


def log_sum(parts):
    peak = jnp.max(parts, axis=0)
    return peak + jnp.log(jnp.sum(jnp.exp(parts - peak[None]), axis=0))


def column_kernel(xs_ref, lp_ref, log_a_ref, *refs, groups):
    y_refs, (r_ref, lt_ref, x1, x2, rows_ref) = refs[:groups], refs[groups:]
    ys = pieces_of(y_refs)
    rows = x1.shape[0]
    spread(xs_ref, x1, x2)
    r = log_a_ref[...] - log_sum(lp_ref[...])
    r_ref[...] = r
    shift = jnp.max(r)
    for k in range(rows // LANES):
        rows_ref[pl.ds(k * LANES, LANES), :] = lanes_to_rows(r[k : k + 1] - shift)
    chunk = 512

    def scores(x, m, y, chunk):
        at = pl.ds(m * chunk, chunk)
        z = times(x[at, :], y)
        return z + wide(rows_ref[at, :], y.shape[0])

    least, most = jnp.float32(1.0), jnp.float32(1.0)
    for first in range(0, len(ys), 4):
        y = jnp.concatenate([ys[first + k][pl.ds(0, PACKED), :] for k in range(4)], axis=0)
        for side, x in enumerate((x1, x2)):
            acc = jnp.zeros((8, 4 * PACKED), F32)
            for m in range(rows // chunk):
                acc += fold(jnp.exp(scores(x, m, y, chunk)), jnp.sum)
            total = jnp.sum(acc, axis=0, keepdims=True)
            lt = shift + jnp.log(total)
            for k in range(4):
                lt_ref[first + k, pl.ds(side, 1), :] = lt[:, k * PACKED : (k + 1) * PACKED]
            least = jnp.minimum(least, jnp.min(total))
            most = jnp.maximum(most, jnp.max(total))

    @pl.when(jnp.logical_not((least > LOW) & (most < HIGH)))
    def _():
        for p in range(len(ys)):
            y = ys[p][pl.ds(0, PACKED), :]
            for side, x in enumerate((x1, x2)):

                def top(m, peak):
                    return jnp.maximum(peak, fold(scores(x, m, y, 256), jnp.max))

                peak = lax.fori_loop(0, rows // 256, top, jnp.full((8, PACKED), -1e30, F32))
                peak = jnp.max(peak, axis=0, keepdims=True)

                def add(m, acc):
                    return acc + fold(jnp.exp(scores(x, m, y, 256) - peak), jnp.sum)

                acc = lax.fori_loop(0, rows // 256, add, jnp.zeros((8, PACKED), F32))
                total = jnp.sum(acc, axis=0, keepdims=True)
                lt_ref[p, pl.ds(side, 1), :] = shift + peak + jnp.log(total)


def column_pass(xs, lps, log_a, ys):
    peers = xs.shape[0]
    rows = peers * 128
    count = sum(y.shape[0] for y in ys)
    return pl.pallas_call(
        functools.partial(column_kernel, groups=len(ys)),
        out_shape=(
            jax.ShapeDtypeStruct((peers, LANES), F32),
            jax.ShapeDtypeStruct((count, 2, PACKED), F32),
        ),
        scratch_shapes=[
            pltpu.VMEM((rows, LANES), BF16),
            pltpu.VMEM((rows, LANES), BF16),
            pltpu.VMEM((rows, LANES), F32),
        ],
        name="column_pass",
        compiler_params=params(),
        cost_estimate=pl.CostEstimate(
            flops=4 * rows * count * PACKED * 128,
            bytes_accessed=4 * 2**20,
            transcendentals=2 * rows * count * PACKED,
        ),
    )(xs, lps, log_a, *ys)


def finish_kernel(lt_ref, r_ref, log_b_ref, sqx_ref, sqy_ref, at_ref, f_ref, g_ref):
    f_ref[...] = r_ref[pl.ds(at_ref[0], 1), :] + 0.5 * sqx_ref[...]
    g_ref[...] = log_b_ref[at_ref[1]] + 0.5 * sqy_ref[...] - log_sum(lt_ref[...])


def finish(lt, r, log_b, sqx, sqy, at):
    vmem = pl.BlockSpec(memory_space=pltpu.VMEM)
    return pl.pallas_call(
        finish_kernel,
        in_specs=[vmem] * 5 + [pl.BlockSpec(memory_space=pltpu.SMEM)],
        out_shape=(
            jax.ShapeDtypeStruct((1, LANES), F32),
            jax.ShapeDtypeStruct((4, LANES), F32),
        ),
        name="finish",
        compiler_params=params(),
    )(lt, r, log_b, sqx, sqy, at)


def exchange(values, axis, groups=None):
    return lax.all_to_all(values, axis, 0, 0, tiled=True, axis_index_groups=groups)


def to_all(values, axis, peers, groups=None):
    return exchange(jnp.broadcast_to(values[None], (peers,) + values.shape), axis, groups)


def per_device(source, target, log_a, log_b, start_potential):
    rows, cols = lax.axis_size("row"), lax.axis_size("col")
    row, col = lax.axis_index("row"), lax.axis_index("col")
    chips = rows // 2
    xs, ys, sqx, sqy = prepare(source, target, start_potential, cols)

    def along(step):
        pairs = [(2 * x + c, 2 * ((x + step) % chips) + c) for x in range(chips) for c in range(2)]
        return lax.ppermute(ys, "row", pairs)

    same = jnp.stack([ys] + [along(step) for step in range(1, chips)])
    other = lax.ppermute(same, "row", [(i, i ^ 1) for i in range(rows)])
    xs = exchange(xs, "col")

    lp = row_pass(xs, [same, other])
    lps = to_all(lp, "col", cols).reshape(cols, cols, LANES)
    r, lt = column_pass(xs, lps, log_a.reshape(cols, LANES), [same, other])

    chip, core = row // 2, row % 2
    owner = jnp.arange(rows)
    piece = (chip - owner // 2) % chips + chips * ((owner % 2) ^ core)
    lt = jnp.take(lt.reshape(rows, 4, LANES), piece, axis=0)
    lt = exchange(lt, "row")
    f, g = finish(lt, r, log_b.reshape(rows, 4, LANES), sqx, sqy, jnp.stack([col, row]))
    return f.reshape(LANES), g.reshape(4 * LANES)


def solution(mesh):
    placed = (
        P(("row", "col"), None),
        P(("col", "row"), None),
        P("row"),
        P("col"),
        P(("col", "row")),
    )
    return jax.shard_map(
        per_device,
        mesh=mesh,
        in_specs=placed,
        out_specs=(P(("row", "col")), P(("col", "row"))),
        check_vma=False,
    )
```

time: 364 us -> 89.5 us (0.25)
  blocking collectives: 202 us -> 0 us
  other arithmetic: 79.1 us -> 0.83 us
  matrix products: 74.6 us -> 0 us
  starting transfers between devices: 0 us -> 35.5 us
  waiting for transfers between devices: 0 us -> 25.4 us
  Pallas kernels: 0 us -> 23.5 us
    all_gather x7 -> x0, blocking collectives: 202 us -> none  [the longest x4 121 us: merged(): gathered = jax.tree.map(lambda a: lax.all_gather(a, axis), part)]
    reduce_sum x33 -> x0, other arithmetic: 76.6 us -> none  [the longest x8 36.9 us: row_pass(): return (peak, jnp.sum(jnp.exp(scores - peak[:, None]), axis=1))]
    dot_general x16 -> x0, matrix products: 74.6 us -> none  [cost_tile(): dots = jnp.dot(block, target.T, preferred_element_type=jnp.float32)]
    all_to_all x0 -> x3, starting transfers between devices: none -> 28.7 us  [exchange(): lax.all_to_all(values, axis, 0, 0, tiled=True, axis_index_groups=groups)]
    pallas_call x0 -> x4, Pallas kernels: none -> 23.5 us  [the longest x1 10.8 us: row_pass(): pl.pallas_call(functools.partial(row_kernel, groups=len(ys)), out_shape=j...]
    all_to_all x0 -> x3, waiting for transfers between devices: none -> 21.4 us  [exchange(): lax.all_to_all(values, axis, 0, 0, tiled=True, axis_index_groups=groups)]
    ppermute x0 -> x4, starting transfers between devices: none -> 6.78 us  [the longest x3 4.89 us: along(): return lax.ppermute(ys, 'row', pairs)]
    ppermute x0 -> x4, waiting for transfers between devices: none -> 4.05 us  [the longest x3 2.87 us: along(): return lax.ppermute(ys, 'row', pairs)]
  transfers between devices with their start and end apart: 0 -> 7, of which waited for: 0 -> 6; matrix products, arithmetic and copies ran while one was open for 0% -> 0% of each run, Pallas kernels for 0% -> 0%
where the time goes in v1:
time: 89.5 us; the launch traced here: 89.1 us
  starting transfers between devices  35.5 us (40%)
  waiting for transfers between devices  25.4 us (28%)
  Pallas kernels  23.5 us (26%)
  local copies, waits for them, and re-layouts  3.1 us (3%)
    all_to_all x3, starting transfers between devices, exchange(): lax.all_to_all(values, axis, 0, 0, tiled=True, axis_index_groups=groups)  28.7 us
    all_to_all x3, waiting for transfers between devices, exchange(): lax.all_to_all(values, axis, 0, 0, tiled=True, axis_index_groups=groups)  21.4 us
    pallas_call x1, Pallas kernels, row_pass(): pl.pallas_call(functools.partial(row_kernel, groups=len(ys)), out_shape=j...  10.8 us
    pallas_call x1, Pallas kernels, column_pass(): pl.pallas_call(functools.partial(column_kernel, groups=len(ys)), out_shap...  10.7 us
    ppermute x3, starting transfers between devices, along(): return lax.ppermute(ys, 'row', pairs)  4.89 us
    ppermute x3, waiting for transfers between devices, along(): return lax.ppermute(ys, 'row', pairs)  2.87 us
    ppermute x1, starting transfers between devices, per_device(): other = lax.ppermute(same, 'row', [(i, i ^ 1) for i in range(rows)])  1.89 us
  transfers between devices with their start and end apart: 7, of which 6 were waited for; matrix products, arithmetic and copies ran while one was open for 0% of the time, Pallas kernels for 0%

profile of v1, /device:TPU:1, one launch (start us, length us, event | category | flops | bytes accessed | tf_op | source)
XLA Modules:
  0.0 89.1 jit_solution(5412273791041831219)
XLA Ops:
  0.6 0.0 copy-start.3
  0.6 1.0 %copy.8.y_ref = bf16[512,64]{1,0:T(8,128)(2,1)S(1)} copy(bf16[512,64]{0,1:T(8,128)(2,1)} %param.6) | data formatting | bytes 131072 | tf_op args[1]
  1.6 0.0 copy-done.3
  1.6 0.0 copy-start.1
  1.6 0.1 copy.7.x_ref
  1.7 0.6 copy-done.1
  2.3 0.9 %prepare.1 = (bf16[32,64,128]{2,1,0:T(8,128)(2,1)}, bf16[272,128]{1,0:T(8,128)(2,1)S(1)}, f32[1,128]{1,0:T(1,128)S(1)}, f32[4,128]{1,0:T(4,128)S(1)}) custom-call(bf16[128,64]{1,0:T(8,128)(2,1)S(1)} %copy.7.x_ref, bf16[512,64]{1,0:T(8,128)(2,1)S(1)} %copy.8.y_ref, f32[4,128]{1,0:T(4,128)S(1)} %bitcast.15), custom_call_target="tpu_custom_call" | custom-call | tf_op jit(solution)/shard_map/prepare/pallas_call | solution.py:64
  3.2 12.0 %all-to-all-start = ((bf16[32,64,128]{2,1,0:T(8,128)(2,1)}), bf16[32,64,128]{2,1,0:T(8,128)(2,1)S(1)}, u32[]{:S(2)}, u32[]{:S(2)}) async-start(bf16[32,64,128]{2,1,0:T(8,128)(2,1)} %get-tuple-element.10), calls=%async_computation | async-start | bytes 1048576 | tf_op jit(solution)/shard_map/all_to_all | solution.py:269
  15.3 1.3 %collective-permute-start = (bf16[272,128]{1,0:T(8,128)(2,1)S(1)}, bf16[272,128]{1,0:T(8,128)(2,1)S(1)}, u32[]{:S(2)}, u32[]{:S(2)}) collective-permute-start(bf16[272,128]{1,0:T(8,128)(2,1)S(1)} %get-tuple-element.11), channel_id=1, source_target_pairs={{0,64},{32,96},{64,128},{96,160},{128,192},{160,224},{192,0},{224,... | collective-permute-start | bytes 208904 | tf_op jit(solution)/shard_map/ppermute | solution.py:284
  16.6 2.5 %collective-permute-start.1 = (bf16[272,128]{1,0:T(8,128)(2,1)S(1)}, bf16[272,128]{1,0:T(8,128)(2,1)S(1)}, u32[]{:S(2)}, u32[]{:S(2)}) collective-permute-start(bf16[272,128]{1,0:T(8,128)(2,1)S(1)} %get-tuple-element.11), channel_id=1, source_target_pairs={{0,128},{32,160},{64,192},{96,224},{128,0},{160,32},{192,64},{224,... | collective-permute-start | bytes 208904 | tf_op jit(solution)/shard_map/ppermute | solution.py:284
  19.0 1.2 %collective-permute-start.2 = (bf16[272,128]{1,0:T(8,128)(2,1)S(1)}, bf16[272,128]{1,0:T(8,128)(2,1)S(1)}, u32[]{:S(2)}, u32[]{:S(2)}) collective-permute-start(bf16[272,128]{1,0:T(8,128)(2,1)S(1)} %get-tuple-element.11), channel_id=1, source_target_pairs={{0,192},{32,224},{64,0},{96,32},{128,64},{160,96},{192,128},{224,1... | collective-permute-start | bytes 208904 | tf_op jit(solution)/shard_map/ppermute | solution.py:284
  20.2 0.0 collective-permute-done
  20.2 1.4 %collective-permute-done.1 = bf16[272,128]{1,0:T(8,128)(2,1)S(1)} collective-permute-done((bf16[272,128]{1,0:T(8,128)(2,1)S(1)}, bf16[272,128]{1,0:T(8,128)(2,1)S(1)}, u32[]{:S(2)}, u32[]{:S(2)}) %collective-permute-start.1) | collective-permute-done | bytes 69664 | tf_op jit(solution)/shard_map/ppermute | solution.py:284
  21.6 1.5 %collective-permute-done.2 = bf16[272,128]{1,0:T(8,128)(2,1)S(1)} collective-permute-done((bf16[272,128]{1,0:T(8,128)(2,1)S(1)}, bf16[272,128]{1,0:T(8,128)(2,1)S(1)}, u32[]{:S(2)}, u32[]{:S(2)}) %collective-permute-start.2) | collective-permute-done | bytes 69664 | tf_op jit(solution)/shard_map/ppermute | solution.py:284
  23.1 1.9 %collective-permute-start.3 = (bf16[4,272,128]{2,1,0:T(8,128)(2,1)S(1)}, bf16[4,272,128]{2,1,0:T(8,128)(2,1)S(1)}, u32[]{:S(2)}, u32[]{:S(2)}) collective-permute-start(bf16[4,272,128]{2,1,0:T(8,128)(2,1)S(1)} %pad_maximum_fusion.refs_0_), channel_id=1, source_target_pairs={{0,32},{32,0},{64,96},{96,64},{128,160},{160,128},{192,224},{224,1... | collective-permute-start | bytes 835592 | tf_op jit(solution)/shard_map/ppermute | solution.py:287
  25.0 1.2 %collective-permute-done.3.refs_1_ = bf16[4,272,128]{2,1,0:T(8,128)(2,1)S(1)} collective-permute-done((bf16[4,272,128]{2,1,0:T(8,128)(2,1)S(1)}, bf16[4,272,128]{2,1,0:T(8,128)(2,1)S(1)}, u32[]{:S(2)}, u32[]{:S(2)}) %collective-permute-start.3) | collective-permute-done | bytes 278560 | tf_op jit(solution)/shard_map/ppermute | solution.py:287
  26.2 3.4 %all-to-all-done.xs_ref = bf16[32,64,128]{2,1,0:T(8,128)(2,1)S(1)} async-done(((bf16[32,64,128]{2,1,0:T(8,128)(2,1)}), bf16[32,64,128]{2,1,0:T(8,128)(2,1)S(1)}, u32[]{:S(2)}, u32[]{:S(2)}) %all-to-all-start) | async-done | bytes 524320 | tf_op jit(solution)/shard_map/all_to_all | solution.py:269
  29.6 10.8 %row_pass.1 = f32[32,128]{1,0:T(8,128)S(1)} custom-call(bf16[32,64,128]{2,1,0:T(8,128)(2,1)S(1)} %all-to-all-done.xs_ref, bf16[4,272,128]{2,1,0:T(8,128)(2,1)S(1)} %pad_maximum_fusion.refs_0_, bf16[4,272,128]{2,1,0:T(8,128)(2,1)S(1)} %collective-permute-done.3.refs_1_), custom_call_target="tpu_custom_call" | custom-call | flops 4294967296 | bytes 4194304 | tf_op jit(solution)/shard_map/row_pass/pallas_call | solution.py:151
  40.4 0.9 broadcast_in_dim.17
  41.2 7.7 %all-to-all-start.1 = ((f32[32,32,128]{2,1,0:T(8,128)}), f32[32,32,128]{2,1,0:T(8,128)S(1)}, u32[]{:S(2)}, u32[]{:S(2)}) async-start(f32[32,32,128]{2,1,0:T(8,128)} %broadcast_in_dim.17), calls=%async_computation.1 | async-start | bytes 1048576 | tf_op jit(solution)/shard_map/all_to_all | solution.py:269
  48.9 0.0 copy-start.2
  49.0 13.4 %all-to-all-done.1.lp_ref = f32[32,32,128]{2,1,0:T(8,128)S(1)} async-done(((f32[32,32,128]{2,1,0:T(8,128)}), f32[32,32,128]{2,1,0:T(8,128)S(1)}, u32[]{:S(2)}, u32[]{:S(2)}) %all-to-all-start.1) | async-done | bytes 524320 | tf_op jit(solution)/shard_map/all_to_all | solution.py:269
  62.3 0.0 copy-done.2
  62.3 10.7 %column_pass.1 = (f32[32,128]{1,0:T(8,128)S(1)}, f32[8,2,256]{2,1,0:T(2,128)S(1)}) custom-call(bf16[32,64,128]{2,1,0:T(8,128)(2,1)S(1)} %all-to-all-done.xs_ref, f32[32,32,128]{2,1,0:T(8,128)S(1)} %all-to-all-done.1.lp_ref, f32[32,128]{1,0:T(8,128)S(1)} %bitcast.16, bf16[4,272,128]{2,1,0:T(8,128)(2,1)S(1)} %pad_maximum_fusion.refs_0_, ...), custom_call_target="tpu_custom_call" | custom-call | flops 4294967296 | bytes 4194304 | tf_op jit(solution)/shard_map/column_pass/pallas_call | solution.py:228
  73.0 0.6 gather_fusion
  73.6 0.7 broadcast_select_fusion
  74.3 0.0 copy-start
  74.3 9.0 %all-to-all-start.2 = ((f32[8,4,128]{2,1,0:T(4,128)}), f32[8,4,128]{2,1,0:T(4,128)S(1)}, u32[]{:S(2)}, u32[]{:S(2)}) async-start(f32[8,4,128]{2,1,0:T(4,128)} %broadcast_select_fusion), calls=%async_computation.2 | async-start | bytes 32768 | tf_op jit(solution)/shard_map/all_to_all | solution.py:269
  83.3 0.1 pad_add_fusion.at_ref
  83.4 4.6 %all-to-all-done.2.lt_ref = f32[8,4,128]{2,1,0:T(4,128)S(1)} async-done(((f32[8,4,128]{2,1,0:T(4,128)}), f32[8,4,128]{2,1,0:T(4,128)S(1)}, u32[]{:S(2)}, u32[]{:S(2)}) %all-to-all-start.2) | async-done | bytes 16416 | tf_op jit(solution)/shard_map/all_to_all | solution.py:269
  87.9 0.0 copy-done
  87.9 1.2 %finish.1 = (f32[1,128]{1,0:T(1,128)}, f32[4,128]{1,0:T(4,128)}) custom-call(f32[8,4,128]{2,1,0:T(4,128)S(1)} %all-to-all-done.2.lt_ref, f32[32,128]{1,0:T(8,128)S(1)} %get-tuple-element.13.r_ref, f32[8,4,128]{2,1,0:T(4,128)S(1)} %bitcast.14, f32[1,128]{1,0:T(1,128)S(1)} %get-tuple-element.14.sqx_ref, f32[4,128]{1,0:T(4,128)S(1)} %get-tuple-element.15.sqy_ref, ...), custom_call_target="tpu_custom_call" | custom-call | tf_op jit(solution)/shard_map/finish/pallas_call | solution.py:256
  (5 shorter events, 0.1 us)
Async XLA Ops:
  0.6 1.0 %copy-start.3 = (bf16[128,64]{0,1:T(8,128)(2,1)S(1)}, bf16[128,64]{0,1:T(8,128)(2,1)}, u32[]{:S(2)}) copy-start(bf16[128,64]{0,1:T(8,128)(2,1)} %param.5) | copy-start | bytes 49156
  1.6 0.7 copy-start.1
  3.2 26.4 %all-to-all-start = ((bf16[32,64,128]{2,1,0:T(8,128)(2,1)}), bf16[32,64,128]{2,1,0:T(8,128)(2,1)S(1)}, u32[]{:S(2)}, u32[]{:S(2)}) async-start(bf16[32,64,128]{2,1,0:T(8,128)(2,1)} %get-tuple-element.10), calls=%async_computation | async-start | bytes 1048576 | tf_op jit(solution)/shard_map/all_to_all | solution.py:269
  15.3 4.9 %collective-permute-start = (bf16[272,128]{1,0:T(8,128)(2,1)S(1)}, bf16[272,128]{1,0:T(8,128)(2,1)S(1)}, u32[]{:S(2)}, u32[]{:S(2)}) collective-permute-start(bf16[272,128]{1,0:T(8,128)(2,1)S(1)} %get-tuple-element.11), channel_id=1, source_target_pairs={{0,64},{32,96},{64,128},{96,160},{128,192},{160,224},{192,0},{224,... | collective-permute-start | bytes 208904 | tf_op jit(solution)/shard_map/ppermute | solution.py:284
  16.6 5.0 %collective-permute-start.1 = (bf16[272,128]{1,0:T(8,128)(2,1)S(1)}, bf16[272,128]{1,0:T(8,128)(2,1)S(1)}, u32[]{:S(2)}, u32[]{:S(2)}) collective-permute-start(bf16[272,128]{1,0:T(8,128)(2,1)S(1)} %get-tuple-element.11), channel_id=1, source_target_pairs={{0,128},{32,160},{64,192},{96,224},{128,0},{160,32},{192,64},{224,... | collective-permute-start | bytes 208904 | tf_op jit(solution)/shard_map/ppermute | solution.py:284
  19.0 4.0 %collective-permute-start.2 = (bf16[272,128]{1,0:T(8,128)(2,1)S(1)}, bf16[272,128]{1,0:T(8,128)(2,1)S(1)}, u32[]{:S(2)}, u32[]{:S(2)}) collective-permute-start(bf16[272,128]{1,0:T(8,128)(2,1)S(1)} %get-tuple-element.11), channel_id=1, source_target_pairs={{0,192},{32,224},{64,0},{96,32},{128,64},{160,96},{192,128},{224,1... | collective-permute-start | bytes 208904 | tf_op jit(solution)/shard_map/ppermute | solution.py:284
  23.1 3.1 %collective-permute-start.3 = (bf16[4,272,128]{2,1,0:T(8,128)(2,1)S(1)}, bf16[4,272,128]{2,1,0:T(8,128)(2,1)S(1)}, u32[]{:S(2)}, u32[]{:S(2)}) collective-permute-start(bf16[4,272,128]{2,1,0:T(8,128)(2,1)S(1)} %pad_maximum_fusion.refs_0_), channel_id=1, source_target_pairs={{0,32},{32,0},{64,96},{96,64},{128,160},{160,128},{192,224},{224,1... | collective-permute-start | bytes 835592 | tf_op jit(solution)/shard_map/ppermute | solution.py:287
  41.2 21.1 %all-to-all-start.1 = ((f32[32,32,128]{2,1,0:T(8,128)}), f32[32,32,128]{2,1,0:T(8,128)S(1)}, u32[]{:S(2)}, u32[]{:S(2)}) async-start(f32[32,32,128]{2,1,0:T(8,128)} %broadcast_in_dim.17), calls=%async_computation.1 | async-start | bytes 1048576 | tf_op jit(solution)/shard_map/all_to_all | solution.py:269
  48.9 13.4 %copy-start.2 = (f32[4096]{0:T(1024)S(1)}, f32[4096]{0:T(1024)}, u32[]{:S(2)}) copy-start(f32[4096]{0:T(1024)} %param.7) | copy-start | bytes 49156
  74.3 13.6 %copy-start = (f32[4096]{0:T(1024)S(1)}, f32[4096]{0:T(1024)}, u32[]{:S(2)}) copy-start(f32[4096]{0:T(1024)} %param.8) | copy-start | bytes 49156
  74.3 13.6 %all-to-all-start.2 = ((f32[8,4,128]{2,1,0:T(4,128)}), f32[8,4,128]{2,1,0:T(4,128)S(1)}, u32[]{:S(2)}, u32[]{:S(2)}) async-start(f32[8,4,128]{2,1,0:T(4,128)} %broadcast_select_fusion), calls=%async_computation.2 | async-start | bytes 32768 | tf_op jit(solution)/shard_map/all_to_all | solution.py:269

commit v2 on v1

v2 whole, which is shorter than its diff:
```python
import functools

import jax
import jax.numpy as jnp
from jax import lax
from jax.experimental import pallas as pl
from jax.experimental.pallas import tpu as pltpu
from jax.sharding import PartitionSpec as P

F32 = jnp.float32
BF16 = jnp.bfloat16
LANES = 128
PACKED = 256
PIECE = PACKED + 16
LOW, HIGH = 1e-24, 1e36


def params(mib=16):
    return pltpu.CompilerParams(vmem_limit_bytes=mib * 2**20)


def lanes_to_rows(values):
    return jnp.broadcast_to(values, (LANES, LANES)).T


def times(left, right):
    return lax.dot_general(left, right, (((1,), (1,)), ((), ())), preferred_element_type=F32)


def wide(rows, columns):
    return jnp.concatenate([rows] * (columns // LANES), axis=1)


def fold(values, combine):
    rows, columns = values.shape
    return combine(values.reshape(rows // 8, 8, columns), axis=0)


def prepare_kernel(
    xt_hbm, yt_hbm, g_hbm, xs_ref, ys_ref, sqx_ref, sqy_ref, part_ref, xt_ref, yt_ref, g_ref, sems
):
    copies = [
        pltpu.make_async_copy(src, dst, sems.at[k])
        for k, (src, dst) in enumerate(((xt_hbm, xt_ref), (yt_hbm, yt_ref), (g_hbm, g_ref)))
    ]
    for copy in copies:
        copy.start()
    for copy in copies:
        copy.wait()
    xt = xt_ref[...].astype(F32)
    x = xt.T.astype(BF16)
    xs_ref[...] = jnp.concatenate([x[:64], x[64:]], axis=1)
    sqx_ref[...] = jnp.sum(xt * xt, axis=0, keepdims=True)
    yt = yt_ref[...].astype(F32)
    y = yt.T.astype(BF16)
    ys_ref[pl.ds(0, PACKED), :] = jnp.concatenate([y[:PACKED], y[PACKED:]], axis=1)
    sqy = jnp.sum(yt * yt, axis=0, keepdims=True)
    part_ref[...] = jnp.zeros_like(part_ref)
    for k in range(4):
        own = sqy[:, k * LANES : (k + 1) * LANES]
        sqy_ref[pl.ds(k, 1), :] = own
        rest = g_ref[pl.ds(k, 1), :] - 0.5 * own
        for level in range(3):
            part = rest.astype(BF16).astype(F32)
            part_ref[pl.ds(4 * level + k, 1), :] = part
            rest = rest - part
    ys_ref[pl.ds(PACKED, 16), :] = part_ref[...].astype(BF16)


def prepare(source, target, g):
    return pl.pallas_call(
        prepare_kernel,
        out_shape=(
            jax.ShapeDtypeStruct((64, LANES), BF16),
            jax.ShapeDtypeStruct((PIECE, LANES), BF16),
            jax.ShapeDtypeStruct((1, LANES), F32),
            jax.ShapeDtypeStruct((4, LANES), F32),
        ),
        in_specs=[pl.BlockSpec(memory_space=pltpu.MemorySpace.HBM)] * 3,
        scratch_shapes=[
            pltpu.VMEM((16, LANES), F32),
            pltpu.VMEM(source.shape[::-1], BF16),
            pltpu.VMEM(target.shape[::-1], BF16),
            pltpu.VMEM((4, LANES), F32),
            pltpu.SemaphoreType.DMA((3,)),
        ],
        name="prepare",
        compiler_params=params(60),
    )(source.T, target.T, g.reshape(4, LANES))


def pair_kernel(xs_ref, far_ref, both_ref):
    peers = both_ref.shape[0]
    second = lax.axis_index("col") // (2 * peers)
    for peer in range(peers):
        both_ref[peer, second] = xs_ref[...]
        both_ref[peer, 1 - second] = far_ref[...]


def pair(xs, far, peers):
    return pl.pallas_call(
        pair_kernel,
        out_shape=jax.ShapeDtypeStruct((peers, 2) + xs.shape, BF16),
        name="pair",
        compiler_params=params(),
    )(xs, far)


def spread(xs_ref, x1, x2):
    zeros = jnp.zeros((64, 64), BF16)
    peers = xs_ref.shape[0]
    for q in range(2 * peers):
        both = xs_ref[q % peers, q // peers]
        top, low = both[:, :64], both[:, 64:]
        x1[pl.ds(q * 128, 64), :] = jnp.concatenate([top, zeros], axis=1)
        x1[pl.ds(q * 128 + 64, 64), :] = jnp.concatenate([low, zeros], axis=1)
        x2[pl.ds(q * 128, 64), :] = jnp.concatenate([zeros, top], axis=1)
        x2[pl.ds(q * 128 + 64, 64), :] = jnp.concatenate([zeros, low], axis=1)


def pieces_of(refs):
    return [ref.at[k] for ref in refs for k in range(ref.shape[0])]


def row_sums(x1, x2, y_refs, h1, h2, put):
    ys = pieces_of(y_refs)
    rows = x1.shape[0]
    tile = 1024
    terms = []
    for y in ys:
        parts = y[pl.ds(PACKED, 16), :].astype(F32)
        terms.append(parts[0:4] + parts[4:8] + parts[8:12])
    shift = jnp.max(functools.reduce(jnp.maximum, terms))

    def scores(p, x, h, n, columns):
        z = times(ys[p][pl.ds(0, PACKED), :], x[pl.ds(n * columns, columns), :])
        return z + wide(h[pl.ds(p * PACKED, PACKED), :], columns)

    least, most = jnp.float32(1.0), jnp.float32(1.0)
    for n in range(rows // tile):
        acc = jnp.zeros((8, tile), F32)
        for p in range(len(ys)):
            if n == 0:
                term = terms[p] - shift
                for k in range(2):
                    at = pl.ds(p * PACKED + k * LANES, LANES)
                    h1[at, :] = lanes_to_rows(term[k : k + 1])
                    h2[at, :] = lanes_to_rows(term[k + 2 : k + 3])
            for x, h in ((x1, h1), (x2, h2)):
                acc += fold(jnp.exp(scores(p, x, h, n, tile)), jnp.sum)
        total = jnp.sum(acc, axis=0, keepdims=True)
        lp = shift + jnp.log(total)
        for k in range(tile // LANES):
            put(n * (tile // LANES) + k, lp[:, k * LANES : (k + 1) * LANES])
        least = jnp.minimum(least, jnp.min(total))
        most = jnp.maximum(most, jnp.max(total))

    @pl.when(jnp.logical_not((least > LOW) & (most < HIGH)))
    def _():
        def exact(n, carry):
            peak = jnp.full((8, LANES), -1e30, F32)
            for p in range(len(ys)):
                for x, h in ((x1, h1), (x2, h2)):
                    peak = jnp.maximum(peak, fold(scores(p, x, h, n, LANES), jnp.max))
            peak = jnp.max(peak, axis=0, keepdims=True)
            acc = jnp.zeros((8, LANES), F32)
            for p in range(len(ys)):
                for x, h in ((x1, h1), (x2, h2)):
                    acc += fold(jnp.exp(scores(p, x, h, n, LANES) - peak), jnp.sum)
            total = jnp.sum(acc, axis=0, keepdims=True)
            put(n, shift + peak + jnp.log(total))
            return carry

        lax.fori_loop(0, rows // LANES, exact, 0)


def joined(first, second):
    top = jnp.maximum(first, second)
    return top + jnp.log(jnp.exp(first - top) + jnp.exp(second - top))


def own_kernel(xs_ref, y_ref, other_ref, lp_ref, x1, x2, h1, h2):
    spread(xs_ref, x1, x2)

    def put(n, values):
        lp_ref[pl.ds(n, 1), :] = values

    row_sums(x1, x2, (y_ref, other_ref), h1, h2, put)


def more_kernel(x1, x2, y_ref, first_ref, lp_ref, h1, h2):
    def put(n, values):
        values = joined(first_ref[pl.ds(n, 1), :], values)
        for peer in range(lp_ref.shape[0]):
            lp_ref[peer, pl.ds(n, 1), :] = values

    row_sums(x1, x2, (y_ref,), h1, h2, put)


def row_cost(rows, packed):
    return pl.CostEstimate(
        flops=4 * rows * packed * 128, bytes_accessed=2**20, transcendentals=2 * rows * packed
    )


def own_rows(xs, ys, other):
    rows, packed = 2 * xs.shape[0] * 128, 2 * ys.shape[0] * PACKED
    return pl.pallas_call(
        own_kernel,
        out_shape=(
            jax.ShapeDtypeStruct((rows // LANES, LANES), F32),
            jax.ShapeDtypeStruct((rows, LANES), BF16),
            jax.ShapeDtypeStruct((rows, LANES), BF16),
        ),
        scratch_shapes=[pltpu.VMEM((packed, LANES), F32)] * 2,
        name="own_rows",
        compiler_params=params(),
        cost_estimate=row_cost(rows, packed),
    )(xs, ys, other)


def more_rows(x1, x2, ys, first, copies):
    rows, packed = x1.shape[0], ys.shape[0] * PACKED
    return pl.pallas_call(
        more_kernel,
        out_shape=jax.ShapeDtypeStruct((copies, rows // LANES, LANES), F32),
        scratch_shapes=[pltpu.VMEM((packed, LANES), F32)] * 2,
        name="more_rows",
        compiler_params=params(),
        cost_estimate=row_cost(rows, packed),
    )(x1, x2, ys, first)


def log_sum(parts):
    peak = jnp.max(parts, axis=0)
    return peak + jnp.log(jnp.sum(jnp.exp(parts - peak[None]), axis=0))


def weights_kernel(lp_ref, log_a_ref, r_ref, rows_ref, shift_ref):
    line = lax.axis_index("col") // log_a_ref.shape[1] % 2
    masses = jnp.concatenate([log_a_ref[line], log_a_ref[line + 2]], axis=0)
    r = masses - log_sum(lp_ref[...])
    r_ref[...] = r
    shift = jnp.max(r)
    shift_ref[...] = jnp.full(shift_ref.shape, shift)
    for k in range(r.shape[0]):
        rows_ref[pl.ds(k * LANES, LANES), :] = lanes_to_rows(r[k : k + 1] - shift)


def column_sums(x1, x2, rows_ref, shift, ys, owners, lt_ref):
    rows = x1.shape[0]
    chunk = 512

    def scores(x, m, y, chunk):
        at = pl.ds(m * chunk, chunk)
        z = times(x[at, :], y)
        return z + wide(rows_ref[at, :], y.shape[0])

    least, most = jnp.float32(1.0), jnp.float32(1.0)
    for first in range(0, len(ys), 4):
        y = jnp.concatenate([ys[first + k][pl.ds(0, PACKED), :] for k in range(4)], axis=0)
        for side, x in enumerate((x1, x2)):
            acc = jnp.zeros((8, 4 * PACKED), F32)
            for m in range(rows // chunk):
                acc += fold(jnp.exp(scores(x, m, y, chunk)), jnp.sum)
            total = jnp.sum(acc, axis=0, keepdims=True)
            lt = shift + jnp.log(total)
            for k in range(4):
                at = pl.ds(side, 1)
                lt_ref[owners[first + k], at, :] = lt[:, k * PACKED : (k + 1) * PACKED]
            least = jnp.minimum(least, jnp.min(total))
            most = jnp.maximum(most, jnp.max(total))

    @pl.when(jnp.logical_not((least > LOW) & (most < HIGH)))
    def _():
        for p in range(len(ys)):
            y = ys[p][pl.ds(0, PACKED), :]
            for side, x in enumerate((x1, x2)):

                def top(m, peak):
                    return jnp.maximum(peak, fold(scores(x, m, y, 256), jnp.max))

                peak = lax.fori_loop(0, rows // 256, top, jnp.full((8, PACKED), -1e30, F32))
                peak = jnp.max(peak, axis=0, keepdims=True)

                def add(m, acc):
                    return acc + fold(jnp.exp(scores(x, m, y, 256) - peak), jnp.sum)

                acc = lax.fori_loop(0, rows // 256, add, jnp.zeros((8, PACKED), F32))
                total = jnp.sum(acc, axis=0, keepdims=True)
                lt_ref[owners[p], pl.ds(side, 1), :] = shift + peak + jnp.log(total)


def owners_of(count):
    row = lax.axis_index("row")
    chips = count // 2
    chip, core = row // 2, row % 2
    return [
        2 * ((chip + chips - step) % chips) + (core if swap == 0 else 1 - core)
        for swap in range(2)
        for step in range(chips)
    ]


def first_kernel(
    x1, x2, lp_ref, log_a_ref, log_b_ref, sqx_ref, sqy_ref, same, other,
    lt_ref, f_ref, base_ref, rows_ref, shift_ref, r_ref
):
    weights_kernel(lp_ref, log_a_ref, r_ref, rows_ref, shift_ref)
    col, depth = lax.axis_index("col"), r_ref.shape[0] // 2
    at = col // (2 * depth) * depth + col % depth
    f_ref[...] = r_ref[pl.ds(at, 1), :] + 0.5 * sqx_ref[...]
    base_ref[...] = log_b_ref[lax.axis_index("row")] + 0.5 * sqy_ref[...]
    ys = pieces_of((same, other))
    column_sums(x1, x2, rows_ref, shift_ref[:, :1], ys, owners_of(len(ys)), lt_ref)


def second_kernel(x1, x2, rows_ref, shift_ref, same, other, lt_ref):
    ys = pieces_of((same, other))
    column_sums(x1, x2, rows_ref, shift_ref[:, :1], ys, owners_of(len(ys)), lt_ref)


def column_cost(rows, count):
    return pl.CostEstimate(
        flops=4 * rows * count * PACKED * 128,
        bytes_accessed=4 * 2**20,
        transcendentals=2 * rows * count * PACKED,
    )


def first_columns(x1, x2, lps, log_a, log_b, sqx, sqy, same, other):
    rows, count = x1.shape[0], 2 * same.shape[0]
    return pl.pallas_call(
        first_kernel,
        out_shape=(
            jax.ShapeDtypeStruct((count, 2, PACKED), F32),
            jax.ShapeDtypeStruct((1, LANES), F32),
            jax.ShapeDtypeStruct((4, LANES), F32),
            jax.ShapeDtypeStruct((rows, LANES), F32),
            jax.ShapeDtypeStruct((1, LANES), F32),
        ),
        scratch_shapes=[pltpu.VMEM((rows // LANES, LANES), F32)],
        name="first_columns",
        compiler_params=params(),
        cost_estimate=column_cost(rows, count),
    )(x1, x2, lps, log_a, log_b, sqx, sqy, same, other)


def second_columns(x1, x2, weights, shift, same, other):
    rows, count = x1.shape[0], 2 * same.shape[0]
    return pl.pallas_call(
        second_kernel,
        out_shape=jax.ShapeDtypeStruct((count, 2, PACKED), F32),
        name="second_columns",
        compiler_params=params(),
        cost_estimate=column_cost(rows, count),
    )(x1, x2, weights, shift, same, other)


def finish_kernel(lt_ref, base_ref, g_ref):
    g_ref[...] = base_ref[...] - log_sum(lt_ref[...])


def finish(lt, base):
    return pl.pallas_call(
        finish_kernel,
        out_shape=jax.ShapeDtypeStruct((4, LANES), F32),
        name="finish",
        compiler_params=params(),
    )(lt, base)


def exchange(values, axis, groups=None):
    return lax.all_to_all(values, axis, 0, 0, tiled=True, axis_index_groups=groups)


def per_device(source, target, log_a, log_b, start_potential):
    rows, cols = lax.axis_size("row"), lax.axis_size("col")
    chips, half, depth = rows // 2, cols // 2, cols // 4
    xs, ys, sqx, sqy = prepare(source, target, start_potential)

    alike = [[2 * y * depth + k + j for y in range(2) for j in range(depth)] for k in (0, depth)]

    def partner(values):
        return lax.ppermute(values, "col", [(i, i ^ depth) for i in range(cols)])

    def along(values, step):
        pairs = [(2 * x + c, 2 * ((x + step) % chips) + c) for x in range(chips) for c in range(2)]
        return lax.ppermute(values, "row", pairs)

    def swap(values):
        return lax.ppermute(values, "row", [(i, i ^ 1) for i in range(rows)])

    own = jnp.stack([ys] + [along(ys, step) for step in range(1, chips)])
    away = partner(own)
    own_other = swap(own)
    far = lax.ppermute(xs, "col", [(i, (i + half) % cols) for i in range(cols)])
    quarters = [list(range(k, k + depth)) for k in range(0, cols, depth)]
    xs = exchange(pair(xs, far, depth), "col", quarters)
    lp, x1, x2 = own_rows(xs, own, own_other)
    away, lp = lax.optimization_barrier((away, lp))
    away_other = swap(away)
    lp = more_rows(x1, x2, away, lp, 1).reshape(lp.shape)
    lps = more_rows(x1, x2, away_other, lp, half)
    lps = exchange(lps, "col", alike)
    log_a, log_b = log_a.reshape(4, depth, LANES), log_b.reshape(rows, 4, LANES)
    lt_away, f, base, weights, shift = first_columns(
        x1, x2, lps, log_a, log_b, sqx, sqy, away, away_other
    )
    lt_back = partner(lt_away)
    lt = second_columns(x1, x2, weights, shift, own, own_other)
    lt = joined(lt, lt_back)
    lt = exchange(lt, "row").reshape(rows, 4, LANES)
    g = finish(lt, base)
    return f.reshape(LANES), g.reshape(4 * LANES)


def solution(mesh):
    placed = (
        P(("row", "col"), None),
        P(("col", "row"), None),
        P("row"),
        P("col"),
        P(("col", "row")),
    )
    return jax.shard_map(
        per_device,
        mesh=mesh,
        in_specs=placed,
        out_specs=(P(("row", "col")), P(("col", "row"))),
        check_vma=False,
    )
```

time: 89.5 us -> 77.8 us (0.87)
  blocking collectives: 0 us -> 21.4 us
  waiting for transfers between devices: 25.4 us -> 6.56 us
  starting transfers between devices: 35.5 us -> 22.6 us
  local copies, waits for them, and re-layouts: 3.1 us -> 1.43 us
  Pallas kernels: 23.5 us -> 24.5 us
    all_to_all x0 -> x2, blocking collectives: none -> 21.4 us  [exchange(): lax.all_to_all(values, axis, 0, 0, tiled=True, axis_index_groups=groups)]
    all_to_all x3 -> x1, starting transfers between devices: 28.7 us -> 8.32 us  [exchange(): lax.all_to_all(values, axis, 0, 0, tiled=True, axis_index_groups=groups)]
    all_to_all x3 -> x1, waiting for transfers between devices: 21.4 us -> 5.78 us  [exchange(): lax.all_to_all(values, axis, 0, 0, tiled=True, axis_index_groups=groups)]
    ppermute x4 -> x8, starting transfers between devices: 6.78 us -> 14.3 us  [the longest x2 6.05 us: swap(): return lax.ppermute(values, 'row', [(i, i ^ 1) for i in range(rows)])]
    ppermute x4 -> x8, waiting for transfers between devices: 4.05 us -> 0.79 us  [the longest x2 0.77 us: swap(): return lax.ppermute(values, 'row', [(i, i ^ 1) for i in range(rows)])]
    pallas_call x4 -> x8, Pallas kernels: 23.5 us -> 24.5 us  [the longest x1 5.92 us: first_columns(): pl.pallas_call(first_kernel, out_shape=(jax.ShapeDtypeStruct((count, 2, P...]
  transfers between devices with their start and end apart: 7 -> 9, of which waited for: 6 -> 2; matrix products, arithmetic and copies ran while one was open for 0% -> 0% of each run, Pallas kernels for 0% -> 17%
where the time goes in v2:
time: 77.8 us; the launch traced here: 77.4 us
  Pallas kernels  24.5 us (31%)
  starting transfers between devices  22.6 us (29%)
  blocking collectives  21.4 us (28%)
  waiting for transfers between devices  6.56 us (8%)
  local copies, waits for them, and re-layouts  1.43 us (2%)
    all_to_all x2, blocking collectives, exchange(): lax.all_to_all(values, axis, 0, 0, tiled=True, axis_index_groups=groups)  21.4 us
    all_to_all x1, starting transfers between devices, exchange(): lax.all_to_all(values, axis, 0, 0, tiled=True, axis_index_groups=groups)  8.32 us
    ppermute x2, starting transfers between devices, swap(): return lax.ppermute(values, 'row', [(i, i ^ 1) for i in range(rows)])  6.05 us
    pallas_call x1, Pallas kernels, first_columns(): pl.pallas_call(first_kernel, out_shape=(jax.ShapeDtypeStruct((count, 2, P...  5.92 us
    all_to_all x1, waiting for transfers between devices, exchange(): lax.all_to_all(values, axis, 0, 0, tiled=True, axis_index_groups=groups)  5.78 us
    pallas_call x2, Pallas kernels, more_rows(): pl.pallas_call(more_kernel, out_shape=jax.ShapeDtypeStruct((copies, rows...  5.63 us
    pallas_call x1, Pallas kernels, own_rows(): pl.pallas_call(own_kernel, out_shape=(jax.ShapeDtypeStruct((rows // LANES...  5.22 us
    pallas_call x1, Pallas kernels, second_columns(): pl.pallas_call(second_kernel, out_shape=jax.ShapeDtypeStruct((count, 2, P...  4.7 us
  transfers between devices with their start and end apart: 9, of which 2 were waited for; matrix products, arithmetic and copies ran while one was open for 0% of the time, Pallas kernels for 17%

profile of v2, /device:TPU:1, one launch (start us, length us, event | category | flops | bytes accessed | tf_op | source)
XLA Modules:
  0.0 77.4 jit_solution(4014447400640959952)
XLA Ops:
  0.6 1.7 %prepare.1 = (bf16[64,128]{1,0:T(8,128)(2,1)}, bf16[272,128]{1,0:T(8,128)(2,1)}, f32[1,128]{1,0:T(1,128)}, f32[4,128]{1,0:T(4,128)}) custom-call(bf16[64,128]{1,0:T(8,128)(2,1)} %bitcast.26, bf16[64,512]{1,0:T(8,128)(2,1)} %bitcast.24, f32[4,128]{1,0:T(4,128)} %bitcast.28), custom_call_target="tpu_custom_call" | custom-call | tf_op jit(solution)/shard_map/prepare/pallas_call | solution.py:71
  2.4 3.8 %collective-permute-start = (bf16[64,128]{1,0:T(8,128)(2,1)}, bf16[64,128]{1,0:T(8,128)(2,1)S(1)}, u32[]{:S(2)}, u32[]{:S(2)}) collective-permute-start(bf16[64,128]{1,0:T(8,128)(2,1)} %get-tuple-element.16.xs_ref), channel_id=1, source_target_pairs={{0,16},{1,17},{2,18},{3,19},{4,20},{5,21},{6,22},{7,23},{8,24},{9,... | collective-permute-start | bytes 49160 | tf_op jit(solution)/shard_map/ppermute | solution.py:397
  6.2 2.5 %collective-permute-start.3 = (bf16[272,128]{1,0:T(8,128)(2,1)}, bf16[272,128]{1,0:T(8,128)(2,1)S(1)}, u32[]{:S(2)}, u32[]{:S(2)}) collective-permute-start(bf16[272,128]{1,0:T(8,128)(2,1)} %get-tuple-element.17), channel_id=1, source_target_pairs={{0,192},{32,224},{64,0},{96,32},{128,64},{160,96},{192,128},{224,1... | collective-permute-start | bytes 208904 | tf_op jit(solution)/shard_map/ppermute | solution.py:389
  8.7 0.5 collective-permute-start.2
  9.2 0.6 collective-permute-start.1
  9.8 0.0 collective-permute-done.far_ref
  9.8 0.7 copy-done
  10.5 0.7 pair.1
  11.3 8.3 %all-to-all-start = ((bf16[8,2,64,128]{3,2,1,0:T(8,128)(2,1)}), bf16[8,2,64,128]{3,2,1,0:T(8,128)(2,1)S(1)}, u32[]{:S(2)}, u32[]{:S(2)}) async-start(bf16[8,2,64,128]{3,2,1,0:T(8,128)(2,1)} %pair.1), calls=%async_computation | async-start | bytes 524288 | tf_op jit(solution)/shard_map/all_to_all | solution.py:374
  19.6 0.0 collective-permute-done.3
  19.6 0.0 collective-permute-done.2
  19.6 0.0 collective-permute-done.1
  19.7 2.2 %collective-permute-start.4 = (bf16[4,272,128]{2,1,0:T(8,128)(2,1)S(1)}, bf16[4,272,128]{2,1,0:T(8,128)(2,1)S(1)}, u32[]{:S(2)}, u32[]{:S(2)}) collective-permute-start(bf16[4,272,128]{2,1,0:T(8,128)(2,1)S(1)} %pad_maximum_fusion.y_ref.same), channel_id=1, source_target_pairs={{0,32},{32,0},{64,96},{96,64},{128,160},{160,128},{192,224},{224,1... | collective-permute-start | bytes 835592 | tf_op jit(solution)/shard_map/ppermute | solution.py:392
  21.8 0.4 collective-permute-start.5
  22.2 0.8 collective-permute-done.4.other_ref.other
  23.0 5.8 %all-to-all-done.xs_ref = bf16[8,2,64,128]{3,2,1,0:T(8,128)(2,1)S(1)} async-done(((bf16[8,2,64,128]{3,2,1,0:T(8,128)(2,1)}), bf16[8,2,64,128]{3,2,1,0:T(8,128)(2,1)S(1)}, u32[]{:S(2)}, u32[]{:S(2)}) %all-to-all-start) | async-done | bytes 262176 | tf_op jit(solution)/shard_map/all_to_all | solution.py:374
  28.8 5.2 %own_rows.1 = (f32[16,128]{1,0:T(8,128)S(1)}, bf16[2048,128]{1,0:T(8,128)(2,1)S(1)}, bf16[2048,128]{1,0:T(8,128)(2,1)S(1)}) custom-call(bf16[8,2,64,128]{3,2,1,0:T(8,128)(2,1)S(1)} %all-to-all-done.xs_ref, bf16[4,272,128]{2,1,0:T(8,128)(2,1)S(1)} %pad_maximum_fusion.y_ref.same, bf16[4,272,128]{2,1,0:T(8,128)(2,1)S(1)} %collective-permute-done.4.other_ref.other), custom_call_target="tpu_custom_call" | custom-call | flops 2147483648 | bytes 1048576 | tf_op jit(solution)/shard_map/own_rows/pallas_call | solution.py:208
  34.0 0.0 collective-permute-done.5.y_ref.same
  34.0 3.9 %collective-permute-start.6 = (bf16[4,272,128]{2,1,0:T(8,128)(2,1)S(1)}, bf16[4,272,128]{2,1,0:T(8,128)(2,1)S(1)}, u32[]{:S(2)}, u32[]{:S(2)}) collective-permute-start(bf16[4,272,128]{2,1,0:T(8,128)(2,1)S(1)} %collective-permute-done.5.y_ref.same), channel_id=1, source_target_pairs={{0,32},{32,0},{64,96},{96,64},{128,160},{160,128},{192,224},{224,1... | collective-permute-start | bytes 835592 | tf_op jit(solution)/shard_map/ppermute | solution.py:392
  37.9 2.8 %more_rows.2 = f32[1,16,128]{2,1,0:T(8,128)S(1)} custom-call(bf16[2048,128]{1,0:T(8,128)(2,1)S(1)} %get-tuple-element.18.x1, bf16[2048,128]{1,0:T(8,128)(2,1)S(1)} %get-tuple-element.19.x2, bf16[4,272,128]{2,1,0:T(8,128)(2,1)S(1)} %collective-permute-done.5.y_ref.same, f32[16,128]{1,0:T(8,128)S(1)} %get-tuple-element.22.first_ref), custom_call_target="tpu_custom_call" | custom-call | flops 1073741824 | bytes 1048576 | tf_op jit(solution)/shard_map/more_rows/pallas_call | solution.py:224
  40.7 0.0 collective-permute-done.6.y_ref.other
  40.7 2.8 %more_rows.3 = f32[16,16,128]{2,1,0:T(8,128)S(1)} custom-call(bf16[2048,128]{1,0:T(8,128)(2,1)S(1)} %get-tuple-element.18.x1, bf16[2048,128]{1,0:T(8,128)(2,1)S(1)} %get-tuple-element.19.x2, bf16[4,272,128]{2,1,0:T(8,128)(2,1)S(1)} %collective-permute-done.6.y_ref.other, f32[16,128]{1,0:T(8,128)S(1)} %bitcast.18), custom_call_target="tpu_custom_call" | custom-call | flops 1073741824 | bytes 1048576 | tf_op jit(solution)/shard_map/more_rows/pallas_call | solution.py:224
  43.6 0.0 copy-start.1
  43.6 0.0 copy-start.2
  43.6 11.6 %all_to_all.15.lp_ref = f32[16,16,128]{2,1,0:T(8,128)S(1)} all-to-all(f32[16,16,128]{2,1,0:T(8,128)S(1)} %more_rows.3), channel_id=1, replica_groups={{0,1,2,3,4,5,6,7,16,17,18,19,20,21,22,23},{8,9,10,11,12,13,14,15,24,25,..., dimensions={0} | all-to-all | bytes 262144 | tf_op jit(solution)/shard_map/all_to_all | solution.py:374
  55.2 0.7 copy-done.3
  55.9 5.9 %first_columns.1 = (f32[8,2,256]{2,1,0:T(2,128)S(1)}, f32[1,128]{1,0:T(1,128)}, f32[4,128]{1,0:T(4,128)S(1)}, f32[2048,128]{1,0:T(8,128)S(1)}, f32[1,128]{1,0:T(1,128)S(1)}) custom-call(bf16[2048,128]{1,0:T(8,128)(2,1)S(1)} %get-tuple-element.18.x1, bf16[2048,128]{1,0:T(8,128)(2,1)S(1)} %get-tuple-element.19.x2, f32[16,16,128]{2,1,0:T(8,128)S(1)} %all_to_all.15.lp_ref, ...), custom_call_target="tpu_custom_call" | custom-call | flops 2147483648 | bytes 4194304 | tf_op jit(solution)/shard_map/first_columns/pallas_call | solution.py:333
  61.8 0.4 collective-permute-start.7
  62.2 4.7 %second_columns.1 = f32[8,2,256]{2,1,0:T(2,128)S(1)} custom-call(bf16[2048,128]{1,0:T(8,128)(2,1)S(1)} %get-tuple-element.18.x1, bf16[2048,128]{1,0:T(8,128)(2,1)S(1)} %get-tuple-element.19.x2, f32[2048,128]{1,0:T(8,128)S(1)} %get-tuple-element.26.rows_ref, f32[1,128]{1,0:T(1,128)S(1)} %get-tuple-element.27.shift_ref, ...), custom_call_target="tpu_custom_call" | custom-call | flops 2147483648 | bytes 4194304 | tf_op jit(solution)/shard_map/second_columns/pallas_call | solution.py:351
  66.9 0.0 collective-permute-done.7
  66.9 9.8 %all_to_all.16 = f32[8,2,256]{2,1,0:T(2,128)S(1)} all-to-all(f32[8,2,256]{2,1,0:T(2,128)S(1)} %bitcast.23), channel_id=1, replica_groups=mesh['row'=8,'col'=32] {'row'}, dimensions={0} | all-to-all | bytes 32768 | tf_op jit(solution)/shard_map/all_to_all | solution.py:374
  76.7 0.6 finish.1
  (11 shorter events, 0.1 us)
Async XLA Ops:
  2.4 7.4 %collective-permute-start = (bf16[64,128]{1,0:T(8,128)(2,1)}, bf16[64,128]{1,0:T(8,128)(2,1)S(1)}, u32[]{:S(2)}, u32[]{:S(2)}) collective-permute-start(bf16[64,128]{1,0:T(8,128)(2,1)} %get-tuple-element.16.xs_ref), channel_id=1, source_target_pairs={{0,16},{1,17},{2,18},{3,19},{4,20},{5,21},{6,22},{7,23},{8,24},{9,... | collective-permute-start | bytes 49160 | tf_op jit(solution)/shard_map/ppermute | solution.py:397
  6.2 13.4 %collective-permute-start.3 = (bf16[272,128]{1,0:T(8,128)(2,1)}, bf16[272,128]{1,0:T(8,128)(2,1)S(1)}, u32[]{:S(2)}, u32[]{:S(2)}) collective-permute-start(bf16[272,128]{1,0:T(8,128)(2,1)} %get-tuple-element.17), channel_id=1, source_target_pairs={{0,192},{32,224},{64,0},{96,32},{128,64},{160,96},{192,128},{224,1... | collective-permute-start | bytes 208904 | tf_op jit(solution)/shard_map/ppermute | solution.py:389
  8.7 10.9 %collective-permute-start.2 = (bf16[272,128]{1,0:T(8,128)(2,1)}, bf16[272,128]{1,0:T(8,128)(2,1)S(1)}, u32[]{:S(2)}, u32[]{:S(2)}) collective-permute-start(bf16[272,128]{1,0:T(8,128)(2,1)} %get-tuple-element.17), channel_id=1, source_target_pairs={{0,128},{32,160},{64,192},{96,224},{128,0},{160,32},{192,64},{224,... | collective-permute-start | bytes 208904 | tf_op jit(solution)/shard_map/ppermute | solution.py:389
  9.2 10.4 %collective-permute-start.1 = (bf16[272,128]{1,0:T(8,128)(2,1)}, bf16[272,128]{1,0:T(8,128)(2,1)S(1)}, u32[]{:S(2)}, u32[]{:S(2)}) collective-permute-start(bf16[272,128]{1,0:T(8,128)(2,1)} %get-tuple-element.17), channel_id=1, source_target_pairs={{0,64},{32,96},{64,128},{96,160},{128,192},{160,224},{192,0},{224,... | collective-permute-start | bytes 208904 | tf_op jit(solution)/shard_map/ppermute | solution.py:389
  9.8 0.7 copy-start
  11.3 8.3 %copy-start.5 = (bf16[272,128]{1,0:T(8,128)(2,1)S(1)}, bf16[272,128]{1,0:T(8,128)(2,1)}, u32[]{:S(2)}) copy-start(bf16[272,128]{1,0:T(8,128)(2,1)} %get-tuple-element.17) | copy-start | bytes 208900
  11.3 17.5 %all-to-all-start = ((bf16[8,2,64,128]{3,2,1,0:T(8,128)(2,1)}), bf16[8,2,64,128]{3,2,1,0:T(8,128)(2,1)S(1)}, u32[]{:S(2)}, u32[]{:S(2)}) async-start(bf16[8,2,64,128]{3,2,1,0:T(8,128)(2,1)} %pair.1), calls=%async_computation | async-start | bytes 524288 | tf_op jit(solution)/shard_map/all_to_all | solution.py:374
  19.7 3.3 %collective-permute-start.4 = (bf16[4,272,128]{2,1,0:T(8,128)(2,1)S(1)}, bf16[4,272,128]{2,1,0:T(8,128)(2,1)S(1)}, u32[]{:S(2)}, u32[]{:S(2)}) collective-permute-start(bf16[4,272,128]{2,1,0:T(8,128)(2,1)S(1)} %pad_maximum_fusion.y_ref.same), channel_id=1, source_target_pairs={{0,32},{32,0},{64,96},{96,64},{128,160},{160,128},{192,224},{224,1... | collective-permute-start | bytes 835592 | tf_op jit(solution)/shard_map/ppermute | solution.py:392
  21.8 12.2 %collective-permute-start.5 = (bf16[4,272,128]{2,1,0:T(8,128)(2,1)S(1)}, bf16[4,272,128]{2,1,0:T(8,128)(2,1)S(1)}, u32[]{:S(2)}, u32[]{:S(2)}) collective-permute-start(bf16[4,272,128]{2,1,0:T(8,128)(2,1)S(1)} %pad_maximum_fusion.y_ref.same), channel_id=1, source_target_pairs={{0,8},{1,9},{2,10},{3,11},{4,12},{5,13},{6,14},{7,15},{8,0},{9,1},... | collective-permute-start | bytes 835592 | tf_op jit(solution)/shard_map/ppermute | solution.py:385
  34.0 6.7 %collective-permute-start.6 = (bf16[4,272,128]{2,1,0:T(8,128)(2,1)S(1)}, bf16[4,272,128]{2,1,0:T(8,128)(2,1)S(1)}, u32[]{:S(2)}, u32[]{:S(2)}) collective-permute-start(bf16[4,272,128]{2,1,0:T(8,128)(2,1)S(1)} %collective-permute-done.5.y_ref.same), channel_id=1, source_target_pairs={{0,32},{32,0},{64,96},{96,64},{128,160},{160,128},{192,224},{224,1... | collective-permute-start | bytes 835592 | tf_op jit(solution)/shard_map/ppermute | solution.py:392
  43.6 11.6 %copy-start.1 = (f32[4096]{0:T(1024)S(1)}, f32[4096]{0:T(1024)}, u32[]{:S(2)}) copy-start(f32[4096]{0:T(1024)} %param.7) | copy-start | bytes 49156
  43.6 11.6 %copy-start.2 = (f32[4096]{0:T(1024)S(1)}, f32[4096]{0:T(1024)}, u32[]{:S(2)}) copy-start(f32[4096]{0:T(1024)} %param.8) | copy-start | bytes 49156
  55.2 0.7 copy-start.3
  55.2 0.7 copy-start.4
  61.8 5.1 %collective-permute-start.7 = (f32[8,2,256]{2,1,0:T(2,128)S(1)}, f32[8,2,256]{2,1,0:T(2,128)S(1)}, u32[]{:S(2)}, u32[]{:S(2)}) collective-permute-start(f32[8,2,256]{2,1,0:T(2,128)S(1)} %get-tuple-element.28), channel_id=1, source_target_pairs={{0,8},{1,9},{2,10},{3,11},{4,12},{5,13},{6,14},{7,15},{8,0},{9,1},... | collective-permute-start | bytes 49160 | tf_op jit(solution)/shard_map/ppermute | solution.py:385

commit v3 on v2

--- a/solution.py
+++ b/solution.py
@@ -36,21 +36,7 @@
     return combine(values.reshape(rows // 8, 8, columns), axis=0)
 
 
-def prepare_kernel(
-    xt_hbm, yt_hbm, g_hbm, xs_ref, ys_ref, sqx_ref, sqy_ref, part_ref, xt_ref, yt_ref, g_ref, sems
-):
-    copies = [
-        pltpu.make_async_copy(src, dst, sems.at[k])
-        for k, (src, dst) in enumerate(((xt_hbm, xt_ref), (yt_hbm, yt_ref), (g_hbm, g_ref)))
-    ]
-    for copy in copies:
-        copy.start()
-    for copy in copies:
-        copy.wait()
-    xt = xt_ref[...].astype(F32)
-    x = xt.T.astype(BF16)
-    xs_ref[...] = jnp.concatenate([x[:64], x[64:]], axis=1)
-    sqx_ref[...] = jnp.sum(xt * xt, axis=0, keepdims=True)
+def prepare_kernel(yt_ref, g_ref, ys_ref, part_ref):
     yt = yt_ref[...].astype(F32)
     y = yt.T.astype(BF16)
     ys_ref[pl.ds(0, PACKED), :] = jnp.concatenate([y[:PACKED], y[PACKED:]], axis=1)
@@ -58,7 +44,6 @@
     part_ref[...] = jnp.zeros_like(part_ref)
     for k in range(4):
         own = sqy[:, k * LANES : (k + 1) * LANES]
-        sqy_ref[pl.ds(k, 1), :] = own
         rest = g_ref[pl.ds(k, 1), :] - 0.5 * own
         for level in range(3):
             part = rest.astype(BF16).astype(F32)
@@ -67,55 +52,30 @@
     ys_ref[pl.ds(PACKED, 16), :] = part_ref[...].astype(BF16)
 
 
-def prepare(source, target, g):
+def prepare(target, g):
     return pl.pallas_call(
         prepare_kernel,
-        out_shape=(
-            jax.ShapeDtypeStruct((64, LANES), BF16),
-            jax.ShapeDtypeStruct((PIECE, LANES), BF16),
-            jax.ShapeDtypeStruct((1, LANES), F32),
-            jax.ShapeDtypeStruct((4, LANES), F32),
-        ),
-        in_specs=[pl.BlockSpec(memory_space=pltpu.MemorySpace.HBM)] * 3,
-        scratch_shapes=[
-            pltpu.VMEM((16, LANES), F32),
-            pltpu.VMEM(source.shape[::-1], BF16),
-            pltpu.VMEM(target.shape[::-1], BF16),
-            pltpu.VMEM((4, LANES), F32),
-            pltpu.SemaphoreType.DMA((3,)),
-        ],
+        out_shape=jax.ShapeDtypeStruct((PIECE, LANES), BF16),
+        scratch_shapes=[pltpu.VMEM((16, LANES), F32)],
         name="prepare",
-        compiler_params=params(60),
-    )(source.T, target.T, g.reshape(4, LANES))
-
-
-def pair_kernel(xs_ref, far_ref, both_ref):
-    peers = both_ref.shape[0]
-    second = lax.axis_index("col") // (2 * peers)
-    for peer in range(peers):
-        both_ref[peer, second] = xs_ref[...]
-        both_ref[peer, 1 - second] = far_ref[...]
-
-
-def pair(xs, far, peers):
-    return pl.pallas_call(
-        pair_kernel,
-        out_shape=jax.ShapeDtypeStruct((peers, 2) + xs.shape, BF16),
-        name="pair",
-        compiler_params=params(),
-    )(xs, far)
+        compiler_params=params(),
+    )(target.T, g.reshape(4, LANES))
+
+
+def pair(one, far, peers):
+    second = lax.axis_index("col") // (2 * peers) == 1
+    both = jnp.stack([jnp.where(second, far, one), jnp.where(second, one, far)])
+    return jnp.broadcast_to(both, (peers,) + both.shape)
 
 
 def spread(xs_ref, x1, x2):
-    zeros = jnp.zeros((64, 64), BF16)
+    zeros = jnp.zeros((LANES, 64), BF16)
     peers = xs_ref.shape[0]
     for q in range(2 * peers):
-        both = xs_ref[q % peers, q // peers]
-        top, low = both[:, :64], both[:, 64:]
-        x1[pl.ds(q * 128, 64), :] = jnp.concatenate([top, zeros], axis=1)
-        x1[pl.ds(q * 128 + 64, 64), :] = jnp.concatenate([low, zeros], axis=1)
-        x2[pl.ds(q * 128, 64), :] = jnp.concatenate([zeros, top], axis=1)
-        x2[pl.ds(q * 128 + 64, 64), :] = jnp.concatenate([zeros, low], axis=1)
+        x = xs_ref[q % peers, q // peers].astype(F32).T.astype(BF16)
+        at = pl.ds(q * LANES, LANES)
+        x1[at, :] = jnp.concatenate([x, zeros], axis=1)
+        x2[at, :] = jnp.concatenate([zeros, x], axis=1)
 
 
 def pieces_of(refs):
@@ -302,22 +262,31 @@
     ]
 
 
-def first_kernel(
-    x1, x2, lp_ref, log_a_ref, log_b_ref, sqx_ref, sqy_ref, same, other,
-    lt_ref, f_ref, base_ref, rows_ref, shift_ref, r_ref
+def first_kernel(x1, x2, lp_ref, log_a_ref, same, other, lt_ref, r_ref, rows_ref, shift_ref):
+    weights_kernel(lp_ref, log_a_ref, r_ref, rows_ref, shift_ref)
+    ys = pieces_of((same, other))
+    column_sums(x1, x2, rows_ref, shift_ref[:, :1], ys, owners_of(len(ys)), lt_ref)
+
+
+def second_kernel(
+    x1, x2, rows_ref, shift_ref, r_ref, same, other, log_b_ref, lt_ref, f_ref, base_ref
 ):
-    weights_kernel(lp_ref, log_a_ref, r_ref, rows_ref, shift_ref)
+    ys = pieces_of((same, other))
+    column_sums(x1, x2, rows_ref, shift_ref[:, :1], ys, owners_of(len(ys)), lt_ref)
     col, depth = lax.axis_index("col"), r_ref.shape[0] // 2
     at = col // (2 * depth) * depth + col % depth
-    f_ref[...] = r_ref[pl.ds(at, 1), :] + 0.5 * sqx_ref[...]
-    base_ref[...] = log_b_ref[lax.axis_index("row")] + 0.5 * sqy_ref[...]
-    ys = pieces_of((same, other))
-    column_sums(x1, x2, rows_ref, shift_ref[:, :1], ys, owners_of(len(ys)), lt_ref)
-
-
-def second_kernel(x1, x2, rows_ref, shift_ref, same, other, lt_ref):
-    ys = pieces_of((same, other))
-    column_sums(x1, x2, rows_ref, shift_ref[:, :1], ys, owners_of(len(ys)), lt_ref)
+    x = x1[pl.ds(pl.multiple_of(at * LANES, LANES), LANES), :].astype(F32).T
+    f_ref[...] = r_ref[pl.ds(at, 1), :] + 0.5 * jnp.sum(x * x, axis=0, keepdims=True)
+    y = same[0, pl.ds(0, PACKED), :].astype(F32).T
+    log_b = log_b_ref[lax.axis_index("row")]
+    for side in range(2):
+        part = y[64 * side : 64 * (side + 1)]
+        sq = jnp.sum(part * part, axis=0, keepdims=True)
+        for k in range(2):
+            row = 2 * side + k
+            base_ref[pl.ds(row, 1), :] = (
+                log_b[row : row + 1] + 0.5 * sq[:, k * LANES : (k + 1) * LANES]
+            )
 
 
 def column_cost(rows, count):
@@ -328,46 +297,52 @@
     )
 
 
-def first_columns(x1, x2, lps, log_a, log_b, sqx, sqy, same, other):
+def first_columns(x1, x2, lps, log_a, same, other):
     rows, count = x1.shape[0], 2 * same.shape[0]
     return pl.pallas_call(
         first_kernel,
+        out_shape=(
+            jax.ShapeDtypeStruct((count, 2, PACKED), F32),
+            jax.ShapeDtypeStruct((rows // LANES, LANES), F32),
+            jax.ShapeDtypeStruct((rows, LANES), F32),
+            jax.ShapeDtypeStruct((1, LANES), F32),
+        ),
+        name="first_columns",
+        compiler_params=params(),
+        cost_estimate=column_cost(rows, count),
+    )(x1, x2, lps, log_a, same, other)
+
+
+def second_columns(x1, x2, weights, shift, r, same, other, log_b):
+    rows, count = x1.shape[0], 2 * same.shape[0]
+    return pl.pallas_call(
+        second_kernel,
         out_shape=(
             jax.ShapeDtypeStruct((count, 2, PACKED), F32),
             jax.ShapeDtypeStruct((1, LANES), F32),
             jax.ShapeDtypeStruct((4, LANES), F32),
-            jax.ShapeDtypeStruct((rows, LANES), F32),
+        ),
+        name="second_columns",
+        compiler_params=params(),
+        cost_estimate=column_cost(rows, count),
+    )(x1, x2, weights, shift, r, same, other, log_b)
+
+
+def finish_kernel(lt_ref, base_ref, own_ref, g_ref, f_ref):
+    g_ref[...] = base_ref[...] - log_sum(lt_ref[...])
+    f_ref[...] = own_ref[...]
+
+
+def finish(lt, base, own):
+    return pl.pallas_call(
+        finish_kernel,
+        out_shape=(
+            jax.ShapeDtypeStruct((4, LANES), F32),
             jax.ShapeDtypeStruct((1, LANES), F32),
         ),
-        scratch_shapes=[pltpu.VMEM((rows // LANES, LANES), F32)],
-        name="first_columns",
-        compiler_params=params(),
-        cost_estimate=column_cost(rows, count),
-    )(x1, x2, lps, log_a, log_b, sqx, sqy, same, other)
-
-
-def second_columns(x1, x2, weights, shift, same, other):
-    rows, count = x1.shape[0], 2 * same.shape[0]
-    return pl.pallas_call(
-        second_kernel,
-        out_shape=jax.ShapeDtypeStruct((count, 2, PACKED), F32),
-        name="second_columns",
-        compiler_params=params(),
-        cost_estimate=column_cost(rows, count),
-    )(x1, x2, weights, shift, same, other)
-
-
-def finish_kernel(lt_ref, base_ref, g_ref):
-    g_ref[...] = base_ref[...] - log_sum(lt_ref[...])
-
-
-def finish(lt, base):
-    return pl.pallas_call(
-        finish_kernel,
-        out_shape=jax.ShapeDtypeStruct((4, LANES), F32),
         name="finish",
         compiler_params=params(),
-    )(lt, base)
+    )(lt, base, own)
 
 
 def exchange(values, axis, groups=None):
@@ -377,7 +352,7 @@
 def per_device(source, target, log_a, log_b, start_potential):
     rows, cols = lax.axis_size("row"), lax.axis_size("col")
     chips, half, depth = rows // 2, cols // 2, cols // 4
-    xs, ys, sqx, sqy = prepare(source, target, start_potential)
+    one, ys = source.T, prepare(target, start_potential)
 
     alike = [[2 * y * depth + k + j for y in range(2) for j in range(depth)] for k in (0, depth)]
 
@@ -394,9 +369,9 @@
     own = jnp.stack([ys] + [along(ys, step) for step in range(1, chips)])
     away = partner(own)
     own_other = swap(own)
-    far = lax.ppermute(xs, "col", [(i, (i + half) % cols) for i in range(cols)])
+    far = lax.ppermute(one, "col", [(i, (i + half) % cols) for i in range(cols)])
     quarters = [list(range(k, k + depth)) for k in range(0, cols, depth)]
-    xs = exchange(pair(xs, far, depth), "col", quarters)
+    xs = exchange(pair(one, far, depth), "col", quarters)
     lp, x1, x2 = own_rows(xs, own, own_other)
     away, lp = lax.optimization_barrier((away, lp))
     away_other = swap(away)
@@ -404,14 +379,12 @@
     lps = more_rows(x1, x2, away_other, lp, half)
     lps = exchange(lps, "col", alike)
     log_a, log_b = log_a.reshape(4, depth, LANES), log_b.reshape(rows, 4, LANES)
-    lt_away, f, base, weights, shift = first_columns(
-        x1, x2, lps, log_a, log_b, sqx, sqy, away, away_other
-    )
+    lt_away, r, weights, shift = first_columns(x1, x2, lps, log_a, away, away_other)
     lt_back = partner(lt_away)
-    lt = second_columns(x1, x2, weights, shift, own, own_other)
+    lt, f, base = second_columns(x1, x2, weights, shift, r, own, own_other, log_b)
     lt = joined(lt, lt_back)
     lt = exchange(lt, "row").reshape(rows, 4, LANES)
-    g = finish(lt, base)
+    g, f = finish(lt, base, f)
     return f.reshape(LANES), g.reshape(4 * LANES)
 
 

time: 77.8 us -> 77.3 us (level)
  Pallas kernels: 24.5 us -> 23.2 us
  local copies, waits for them, and re-layouts: 1.43 us -> 2.33 us
    pallas_call x4 -> x3, Pallas kernels: 7.78 us -> 5.71 us  [the longest x1 4.93 us: second_columns(): pl.pallas_call(second_kernel, out_shape=(jax.ShapeDtypeStruct((count, 2,...]
    unnamed x12 -> x10, local copies, waits for them, and re-layouts: 1.41 us -> 1.57 us
  transfers between devices with their start and end apart: 9 -> 9, of which waited for: 2 -> 2; matrix products, arithmetic and copies ran while one was open for 0% -> 1% of each run, Pallas kernels for 17% -> 18%
where the time goes in v3:
time: 77.3 us; the launch traced here: 76.9 us
  Pallas kernels  23.2 us (30%)
  starting transfers between devices  22.6 us (29%)
  blocking collectives  21.3 us (28%)
  waiting for transfers between devices  6.57 us (8%)
  local copies, waits for them, and re-layouts  2.33 us (3%)
    all_to_all x2, blocking collectives, exchange(): lax.all_to_all(values, axis, 0, 0, tiled=True, axis_index_groups=groups)  21.3 us
    all_to_all x1, starting transfers between devices, exchange(): lax.all_to_all(values, axis, 0, 0, tiled=True, axis_index_groups=groups)  8.19 us
    ppermute x2, starting transfers between devices, swap(): return lax.ppermute(values, 'row', [(i, i ^ 1) for i in range(rows)])  6.05 us
    pallas_call x2, Pallas kernels, more_rows(): pl.pallas_call(more_kernel, out_shape=jax.ShapeDtypeStruct((copies, rows...  5.99 us
    pallas_call x1, Pallas kernels, own_rows(): pl.pallas_call(own_kernel, out_shape=(jax.ShapeDtypeStruct((rows // LANES...  5.93 us
    all_to_all x1, waiting for transfers between devices, exchange(): lax.all_to_all(values, axis, 0, 0, tiled=True, axis_index_groups=groups)  5.79 us
    pallas_call x1, Pallas kernels, first_columns(): pl.pallas_call(first_kernel, out_shape=(jax.ShapeDtypeStruct((count, 2, P...  5.6 us
    pallas_call x1, Pallas kernels, second_columns(): pl.pallas_call(second_kernel, out_shape=(jax.ShapeDtypeStruct((count, 2,...  4.93 us
  transfers between devices with their start and end apart: 9, of which 2 were waited for; matrix products, arithmetic and copies ran while one was open for 1% of the time, Pallas kernels for 18%

profile of v3, /device:TPU:1, one launch (start us, length us, event | category | flops | bytes accessed | tf_op | source)
XLA Modules:
  0.0 76.9 jit_solution(11376697894401115691)
XLA Ops:
  0.6 3.8 %collective-permute-start = (bf16[64,128]{1,0:T(8,128)(2,1)}, bf16[64,128]{1,0:T(8,128)(2,1)S(1)}, u32[]{:S(2)}, u32[]{:S(2)}) collective-permute-start(bf16[64,128]{1,0:T(8,128)(2,1)} %bitcast.33), channel_id=1, source_target_pairs={{0,16},{1,17},{2,18},{3,19},{4,20},{5,21},{6,22},{7,23},{8,24},{9,... | collective-permute-start | bytes 49160 | tf_op jit(solution)/shard_map/ppermute | solution.py:372
  4.5 0.8 %copy-done = bf16[512,64]{0,1:T(8,128)(2,1)S(1)} copy-done((bf16[512,64]{0,1:T(8,128)(2,1)S(1)}, bf16[512,64]{0,1:T(8,128)(2,1)}, u32[]{:S(2)}) %copy-start) | copy-done | bytes 65560
  5.3 0.2 prepare.1
  5.5 2.6 %collective-permute-start.3 = (bf16[272,128]{1,0:T(8,128)(2,1)S(1)}, bf16[272,128]{1,0:T(8,128)(2,1)S(1)}, u32[]{:S(2)}, u32[]{:S(2)}) collective-permute-start(bf16[272,128]{1,0:T(8,128)(2,1)S(1)} %prepare.1), channel_id=1, source_target_pairs={{0,192},{32,224},{64,0},{96,32},{128,64},{160,96},{192,128},{224,1... | collective-permute-start | bytes 208904 | tf_op jit(solution)/shard_map/ppermute | solution.py:364
  8.0 0.5 collective-permute-start.2
  8.6 0.6 collective-permute-start.1
  9.2 0.0 collective-permute-done
  9.2 0.7 copy-done.4
  9.9 0.7 broadcast_in_dim.3
  10.7 8.2 %all-to-all-start = ((bf16[8,2,64,128]{3,2,1,0:T(8,128)(2,1)}), bf16[8,2,64,128]{3,2,1,0:T(8,128)(2,1)S(1)}, u32[]{:S(2)}, u32[]{:S(2)}) async-start(bf16[8,2,64,128]{3,2,1,0:T(8,128)(2,1)} %broadcast_in_dim.3), calls=%async_computation | async-start | bytes 524288 | tf_op jit(solution)/shard_map/all_to_all | solution.py:349
  18.8 0.0 collective-permute-done.3
  18.8 0.0 collective-permute-done.2
  18.9 0.0 collective-permute-done.1
  18.9 2.2 %collective-permute-start.4 = (bf16[4,272,128]{2,1,0:T(8,128)(2,1)S(1)}, bf16[4,272,128]{2,1,0:T(8,128)(2,1)S(1)}, u32[]{:S(2)}, u32[]{:S(2)}) collective-permute-start(bf16[4,272,128]{2,1,0:T(8,128)(2,1)S(1)} %pad_maximum_fusion.y_ref.same), channel_id=1, source_target_pairs={{0,32},{32,0},{64,96},{96,64},{128,160},{160,128},{192,224},{224,1... | collective-permute-start | bytes 835592 | tf_op jit(solution)/shard_map/ppermute | solution.py:367
  21.1 0.4 collective-permute-start.5
  21.5 0.8 collective-permute-done.4.other_ref.other
  22.3 5.8 %all-to-all-done.xs_ref = bf16[8,2,64,128]{3,2,1,0:T(8,128)(2,1)S(1)} async-done(((bf16[8,2,64,128]{3,2,1,0:T(8,128)(2,1)}), bf16[8,2,64,128]{3,2,1,0:T(8,128)(2,1)S(1)}, u32[]{:S(2)}, u32[]{:S(2)}) %all-to-all-start) | async-done | bytes 262176 | tf_op jit(solution)/shard_map/all_to_all | solution.py:349
  28.0 5.9 %own_rows.1 = (f32[16,128]{1,0:T(8,128)S(1)}, bf16[2048,128]{1,0:T(8,128)(2,1)S(1)}, bf16[2048,128]{1,0:T(8,128)(2,1)S(1)}) custom-call(bf16[8,2,64,128]{3,2,1,0:T(8,128)(2,1)S(1)} %all-to-all-done.xs_ref, bf16[4,272,128]{2,1,0:T(8,128)(2,1)S(1)} %pad_maximum_fusion.y_ref.same, bf16[4,272,128]{2,1,0:T(8,128)(2,1)S(1)} %collective-permute-done.4.other_ref.other), custom_call_target="tpu_custom_call" | custom-call | flops 2147483648 | bytes 1048576 | tf_op jit(solution)/shard_map/own_rows/pallas_call | solution.py:168
  34.0 0.0 collective-permute-done.5.y_ref.same
  34.0 3.9 %collective-permute-start.6 = (bf16[4,272,128]{2,1,0:T(8,128)(2,1)S(1)}, bf16[4,272,128]{2,1,0:T(8,128)(2,1)S(1)}, u32[]{:S(2)}, u32[]{:S(2)}) collective-permute-start(bf16[4,272,128]{2,1,0:T(8,128)(2,1)S(1)} %collective-permute-done.5.y_ref.same), channel_id=1, source_target_pairs={{0,32},{32,0},{64,96},{96,64},{128,160},{160,128},{192,224},{224,1... | collective-permute-start | bytes 835592 | tf_op jit(solution)/shard_map/ppermute | solution.py:367
  37.9 3.0 %more_rows.2 = f32[1,16,128]{2,1,0:T(8,128)S(1)} custom-call(bf16[2048,128]{1,0:T(8,128)(2,1)S(1)} %get-tuple-element.16.x1, bf16[2048,128]{1,0:T(8,128)(2,1)S(1)} %get-tuple-element.17.x2, bf16[4,272,128]{2,1,0:T(8,128)(2,1)S(1)} %collective-permute-done.5.y_ref.same, f32[16,128]{1,0:T(8,128)S(1)} %get-tuple-element.20.first_ref), custom_call_target="tpu_custom_call" | custom-call | flops 1073741824 | bytes 1048576 | tf_op jit(solution)/shard_map/more_rows/pallas_call | solution.py:184
  40.9 0.0 collective-permute-done.6.y_ref.other
  40.9 3.0 %more_rows.3 = f32[16,16,128]{2,1,0:T(8,128)S(1)} custom-call(bf16[2048,128]{1,0:T(8,128)(2,1)S(1)} %get-tuple-element.16.x1, bf16[2048,128]{1,0:T(8,128)(2,1)S(1)} %get-tuple-element.17.x2, bf16[4,272,128]{2,1,0:T(8,128)(2,1)S(1)} %collective-permute-done.6.y_ref.other, f32[16,128]{1,0:T(8,128)S(1)} %bitcast.27), custom_call_target="tpu_custom_call" | custom-call | flops 1073741824 | bytes 1048576 | tf_op jit(solution)/shard_map/more_rows/pallas_call | solution.py:184
  43.9 0.0 copy-start.2
  43.9 11.6 %all_to_all.15.lp_ref = f32[16,16,128]{2,1,0:T(8,128)S(1)} all-to-all(f32[16,16,128]{2,1,0:T(8,128)S(1)} %more_rows.3), channel_id=1, replica_groups={{0,1,2,3,4,5,6,7,16,17,18,19,20,21,22,23},{8,9,10,11,12,13,14,15,24,25,..., dimensions={0} | all-to-all | bytes 262144 | tf_op jit(solution)/shard_map/all_to_all | solution.py:349
  55.5 0.0 copy-done.2
  55.5 5.6 %first_columns.1 = (f32[8,2,256]{2,1,0:T(2,128)S(1)}, f32[16,128]{1,0:T(8,128)S(1)}, f32[2048,128]{1,0:T(8,128)S(1)}, f32[1,128]{1,0:T(1,128)S(1)}) custom-call(bf16[2048,128]{1,0:T(8,128)(2,1)S(1)} %get-tuple-element.16.x1, bf16[2048,128]{1,0:T(8,128)(2,1)S(1)} %get-tuple-element.17.x2, f32[16,16,128]{2,1,0:T(8,128)S(1)} %all_to_all.15.lp_ref, ...), custom_call_target="tpu_custom_call" | custom-call | flops 2147483648 | bytes 4194304 | tf_op jit(solution)/shard_map/first_columns/pallas_call | solution.py:302
  61.1 0.5 collective-permute-start.7
  61.6 4.9 %second_columns.1 = (f32[8,2,256]{2,1,0:T(2,128)S(1)}, f32[1,128]{1,0:T(1,128)S(1)}, f32[4,128]{1,0:T(4,128)S(1)}) custom-call(bf16[2048,128]{1,0:T(8,128)(2,1)S(1)} %get-tuple-element.16.x1, bf16[2048,128]{1,0:T(8,128)(2,1)S(1)} %get-tuple-element.17.x2, f32[2048,128]{1,0:T(8,128)S(1)} %get-tuple-element.21.rows_ref, ...), custom_call_target="tpu_custom_call" | custom-call | flops 2147483648 | bytes 4194304 | tf_op jit(solution)/shard_map/second_columns/pallas_call | solution.py:318
  66.5 0.0 collective-permute-done.7
  66.6 9.7 %all_to_all.16 = f32[8,2,256]{2,1,0:T(2,128)S(1)} all-to-all(f32[8,2,256]{2,1,0:T(2,128)S(1)} %bitcast.31), channel_id=1, replica_groups=mesh['row'=8,'col'=32] {'row'}, dimensions={0} | all-to-all | bytes 32768 | tf_op jit(solution)/shard_map/all_to_all | solution.py:349
  76.3 0.6 finish.1
  (11 shorter events, 0.1 us)
Async XLA Ops:
  0.6 3.8 %copy-start.1 = (f32[512]{0:T(512)S(1)}, f32[512]{0:T(512)}, u32[]{:S(2)}) copy-start(f32[512]{0:T(512)} %param.9) | copy-start | bytes 6148
  0.6 8.5 %collective-permute-start = (bf16[64,128]{1,0:T(8,128)(2,1)}, bf16[64,128]{1,0:T(8,128)(2,1)S(1)}, u32[]{:S(2)}, u32[]{:S(2)}) collective-permute-start(bf16[64,128]{1,0:T(8,128)(2,1)} %bitcast.33), channel_id=1, source_target_pairs={{0,16},{1,17},{2,18},{3,19},{4,20},{5,21},{6,22},{7,23},{8,24},{9,... | collective-permute-start | bytes 49160 | tf_op jit(solution)/shard_map/ppermute | solution.py:372
  4.5 0.8 %copy-start = (bf16[512,64]{0,1:T(8,128)(2,1)S(1)}, bf16[512,64]{0,1:T(8,128)(2,1)}, u32[]{:S(2)}) copy-start(bf16[512,64]{0,1:T(8,128)(2,1)} %param.6) | copy-start | bytes 196612
  5.5 13.3 %collective-permute-start.3 = (bf16[272,128]{1,0:T(8,128)(2,1)S(1)}, bf16[272,128]{1,0:T(8,128)(2,1)S(1)}, u32[]{:S(2)}, u32[]{:S(2)}) collective-permute-start(bf16[272,128]{1,0:T(8,128)(2,1)S(1)} %prepare.1), channel_id=1, source_target_pairs={{0,192},{32,224},{64,0},{96,32},{128,64},{160,96},{192,128},{224,1... | collective-permute-start | bytes 208904 | tf_op jit(solution)/shard_map/ppermute | solution.py:364
  8.0 10.8 %collective-permute-start.2 = (bf16[272,128]{1,0:T(8,128)(2,1)S(1)}, bf16[272,128]{1,0:T(8,128)(2,1)S(1)}, u32[]{:S(2)}, u32[]{:S(2)}) collective-permute-start(bf16[272,128]{1,0:T(8,128)(2,1)S(1)} %prepare.1), channel_id=1, source_target_pairs={{0,128},{32,160},{64,192},{96,224},{128,0},{160,32},{192,64},{224,... | collective-permute-start | bytes 208904 | tf_op jit(solution)/shard_map/ppermute | solution.py:364
  8.6 10.3 %collective-permute-start.1 = (bf16[272,128]{1,0:T(8,128)(2,1)S(1)}, bf16[272,128]{1,0:T(8,128)(2,1)S(1)}, u32[]{:S(2)}, u32[]{:S(2)}) collective-permute-start(bf16[272,128]{1,0:T(8,128)(2,1)S(1)} %prepare.1), channel_id=1, source_target_pairs={{0,64},{32,96},{64,128},{96,160},{128,192},{160,224},{192,0},{224,... | collective-permute-start | bytes 208904 | tf_op jit(solution)/shard_map/ppermute | solution.py:364
  9.2 0.7 copy-start.4
  10.7 17.4 %all-to-all-start = ((bf16[8,2,64,128]{3,2,1,0:T(8,128)(2,1)}), bf16[8,2,64,128]{3,2,1,0:T(8,128)(2,1)S(1)}, u32[]{:S(2)}, u32[]{:S(2)}) async-start(bf16[8,2,64,128]{3,2,1,0:T(8,128)(2,1)} %broadcast_in_dim.3), calls=%async_computation | async-start | bytes 524288 | tf_op jit(solution)/shard_map/all_to_all | solution.py:349
  18.9 3.3 %collective-permute-start.4 = (bf16[4,272,128]{2,1,0:T(8,128)(2,1)S(1)}, bf16[4,272,128]{2,1,0:T(8,128)(2,1)S(1)}, u32[]{:S(2)}, u32[]{:S(2)}) collective-permute-start(bf16[4,272,128]{2,1,0:T(8,128)(2,1)S(1)} %pad_maximum_fusion.y_ref.same), channel_id=1, source_target_pairs={{0,32},{32,0},{64,96},{96,64},{128,160},{160,128},{192,224},{224,1... | collective-permute-start | bytes 835592 | tf_op jit(solution)/shard_map/ppermute | solution.py:367
  21.1 12.9 %collective-permute-start.5 = (bf16[4,272,128]{2,1,0:T(8,128)(2,1)S(1)}, bf16[4,272,128]{2,1,0:T(8,128)(2,1)S(1)}, u32[]{:S(2)}, u32[]{:S(2)}) collective-permute-start(bf16[4,272,128]{2,1,0:T(8,128)(2,1)S(1)} %pad_maximum_fusion.y_ref.same), channel_id=1, source_target_pairs={{0,8},{1,9},{2,10},{3,11},{4,12},{5,13},{6,14},{7,15},{8,0},{9,1},... | collective-permute-start | bytes 835592 | tf_op jit(solution)/shard_map/ppermute | solution.py:360
  34.0 6.9 %collective-permute-start.6 = (bf16[4,272,128]{2,1,0:T(8,128)(2,1)S(1)}, bf16[4,272,128]{2,1,0:T(8,128)(2,1)S(1)}, u32[]{:S(2)}, u32[]{:S(2)}) collective-permute-start(bf16[4,272,128]{2,1,0:T(8,128)(2,1)S(1)} %collective-permute-done.5.y_ref.same), channel_id=1, source_target_pairs={{0,32},{32,0},{64,96},{96,64},{128,160},{160,128},{192,224},{224,1... | collective-permute-start | bytes 835592 | tf_op jit(solution)/shard_map/ppermute | solution.py:367
  43.9 11.6 %copy-start.2 = (f32[4096]{0:T(1024)S(1)}, f32[4096]{0:T(1024)}, u32[]{:S(2)}) copy-start(f32[4096]{0:T(1024)} %param.7) | copy-start | bytes 49156
  55.5 6.1 %copy-start.3 = (f32[4096]{0:T(1024)S(1)}, f32[4096]{0:T(1024)}, u32[]{:S(2)}) copy-start(f32[4096]{0:T(1024)} %param.8) | copy-start | bytes 49156
  61.1 5.4 %collective-permute-start.7 = (f32[8,2,256]{2,1,0:T(2,128)S(1)}, f32[8,2,256]{2,1,0:T(2,128)S(1)}, u32[]{:S(2)}, u32[]{:S(2)}) collective-permute-start(f32[8,2,256]{2,1,0:T(2,128)S(1)} %get-tuple-element.25), channel_id=1, source_target_pairs={{0,8},{1,9},{2,10},{3,11},{4,12},{5,13},{6,14},{7,15},{8,0},{9,1},... | collective-permute-start | bytes 49160 | tf_op jit(solution)/shard_map/ppermute | solution.py:360

commit v4 on v3

--- a/solution.py
+++ b/solution.py
@@ -36,7 +36,8 @@
     return combine(values.reshape(rows // 8, 8, columns), axis=0)
 
 
-def prepare_kernel(yt_ref, g_ref, ys_ref, part_ref):
+def prepare_kernel(yt_ref, g_ref, xt_ref, ys_ref, one_ref, part_ref):
+    one_ref[...] = xt_ref[...]
     yt = yt_ref[...].astype(F32)
     y = yt.T.astype(BF16)
     ys_ref[pl.ds(0, PACKED), :] = jnp.concatenate([y[:PACKED], y[PACKED:]], axis=1)
@@ -52,27 +53,26 @@
     ys_ref[pl.ds(PACKED, 16), :] = part_ref[...].astype(BF16)
 
 
-def prepare(target, g):
+def prepare(target, g, xt):
     return pl.pallas_call(
         prepare_kernel,
-        out_shape=jax.ShapeDtypeStruct((PIECE, LANES), BF16),
+        out_shape=(
+            jax.ShapeDtypeStruct((PIECE, LANES), BF16),
+            jax.ShapeDtypeStruct(xt.shape, BF16),
+        ),
         scratch_shapes=[pltpu.VMEM((16, LANES), F32)],
         name="prepare",
         compiler_params=params(),
-    )(target.T, g.reshape(4, LANES))
-
-
-def pair(one, far, peers):
-    second = lax.axis_index("col") // (2 * peers) == 1
-    both = jnp.stack([jnp.where(second, far, one), jnp.where(second, one, far)])
-    return jnp.broadcast_to(both, (peers,) + both.shape)
+    )(target.T, g.reshape(4, LANES), xt)
 
 
 def spread(xs_ref, x1, x2):
     zeros = jnp.zeros((LANES, 64), BF16)
     peers = xs_ref.shape[0]
+    half = lax.axis_index("col") // (2 * peers)
     for q in range(2 * peers):
-        x = xs_ref[q % peers, q // peers].astype(F32).T.astype(BF16)
+        side = half if q < peers else 1 - half
+        x = xs_ref[q % peers, side].astype(F32).T.astype(BF16)
         at = pl.ds(q * LANES, LANES)
         x1[at, :] = jnp.concatenate([x, zeros], axis=1)
         x2[at, :] = jnp.concatenate([zeros, x], axis=1)
@@ -82,15 +82,44 @@
     return [ref.at[k] for ref in refs for k in range(ref.shape[0])]
 
 
-def row_sums(x1, x2, y_refs, h1, h2, put):
-    ys = pieces_of(y_refs)
-    rows = x1.shape[0]
-    tile = 1024
+def spread_terms(ys, h1, h2):
     terms = []
     for y in ys:
         parts = y[pl.ds(PACKED, 16), :].astype(F32)
         terms.append(parts[0:4] + parts[4:8] + parts[8:12])
     shift = jnp.max(functools.reduce(jnp.maximum, terms))
+    for p, term in enumerate(terms):
+        term = term - shift
+        for k in range(2):
+            at = pl.ds(p * PACKED + k * LANES, LANES)
+            h1[at, :] = lanes_to_rows(term[k : k + 1])
+            h2[at, :] = lanes_to_rows(term[k + 2 : k + 3])
+    return shift
+
+
+def terms_kernel(y_ref, other_ref, h1, h2, shift_ref):
+    shift = spread_terms(pieces_of((y_ref, other_ref)), h1, h2)
+    shift_ref[...] = jnp.full(shift_ref.shape, shift)
+
+
+def target_terms(ys, other):
+    packed = 2 * ys.shape[0] * PACKED
+    return pl.pallas_call(
+        terms_kernel,
+        out_shape=(
+            jax.ShapeDtypeStruct((packed, LANES), F32),
+            jax.ShapeDtypeStruct((packed, LANES), F32),
+            jax.ShapeDtypeStruct((1, LANES), F32),
+        ),
+        name="target_terms",
+        compiler_params=params(),
+    )(ys, other)
+
+
+def row_sums(x1, x2, y_refs, h1, h2, shift, put):
+    ys = pieces_of(y_refs)
+    rows = x1.shape[0]
+    tile = 1024
 
     def scores(p, x, h, n, columns):
         z = times(ys[p][pl.ds(0, PACKED), :], x[pl.ds(n * columns, columns), :])
@@ -100,12 +129,6 @@
     for n in range(rows // tile):
         acc = jnp.zeros((8, tile), F32)
         for p in range(len(ys)):
-            if n == 0:
-                term = terms[p] - shift
-                for k in range(2):
-                    at = pl.ds(p * PACKED + k * LANES, LANES)
-                    h1[at, :] = lanes_to_rows(term[k : k + 1])
-                    h2[at, :] = lanes_to_rows(term[k + 2 : k + 3])
             for x, h in ((x1, h1), (x2, h2)):
                 acc += fold(jnp.exp(scores(p, x, h, n, tile)), jnp.sum)
         total = jnp.sum(acc, axis=0, keepdims=True)
@@ -139,13 +162,13 @@
     return top + jnp.log(jnp.exp(first - top) + jnp.exp(second - top))
 
 
-def own_kernel(xs_ref, y_ref, other_ref, lp_ref, x1, x2, h1, h2):
+def own_kernel(xs_ref, y_ref, other_ref, h1, h2, shift_ref, lp_ref, x1, x2):
     spread(xs_ref, x1, x2)
 
     def put(n, values):
         lp_ref[pl.ds(n, 1), :] = values
 
-    row_sums(x1, x2, (y_ref, other_ref), h1, h2, put)
+    row_sums(x1, x2, (y_ref, other_ref), h1, h2, shift_ref[:, :1], put)
 
 
 def more_kernel(x1, x2, y_ref, first_ref, lp_ref, h1, h2):
@@ -154,7 +177,8 @@
         for peer in range(lp_ref.shape[0]):
             lp_ref[peer, pl.ds(n, 1), :] = values
 
-    row_sums(x1, x2, (y_ref,), h1, h2, put)
+    shift = spread_terms(pieces_of((y_ref,)), h1, h2)
+    row_sums(x1, x2, (y_ref,), h1, h2, shift, put)
 
 
 def row_cost(rows, packed):
@@ -163,7 +187,7 @@
     )
 
 
-def own_rows(xs, ys, other):
+def own_rows(xs, ys, other, h1, h2, shift):
     rows, packed = 2 * xs.shape[0] * 128, 2 * ys.shape[0] * PACKED
     return pl.pallas_call(
         own_kernel,
@@ -172,11 +196,10 @@
             jax.ShapeDtypeStruct((rows, LANES), BF16),
             jax.ShapeDtypeStruct((rows, LANES), BF16),
         ),
-        scratch_shapes=[pltpu.VMEM((packed, LANES), F32)] * 2,
         name="own_rows",
         compiler_params=params(),
         cost_estimate=row_cost(rows, packed),
-    )(xs, ys, other)
+    )(xs, ys, other, h1, h2, shift)
 
 
 def more_rows(x1, x2, ys, first, copies):
@@ -352,7 +375,7 @@
 def per_device(source, target, log_a, log_b, start_potential):
     rows, cols = lax.axis_size("row"), lax.axis_size("col")
     chips, half, depth = rows // 2, cols // 2, cols // 4
-    one, ys = source.T, prepare(target, start_potential)
+    ys, one = prepare(target, start_potential, source.T)
 
     alike = [[2 * y * depth + k + j for y in range(2) for j in range(depth)] for k in (0, depth)]
 
@@ -369,10 +392,11 @@
     own = jnp.stack([ys] + [along(ys, step) for step in range(1, chips)])
     away = partner(own)
     own_other = swap(own)
-    far = lax.ppermute(one, "col", [(i, (i + half) % cols) for i in range(cols)])
+    far = lax.ppermute(source.T, "col", [(i, (i + half) % cols) for i in range(cols)])
     quarters = [list(range(k, k + depth)) for k in range(0, cols, depth)]
-    xs = exchange(pair(one, far, depth), "col", quarters)
-    lp, x1, x2 = own_rows(xs, own, own_other)
+    both = jnp.stack([one, far])
+    xs = exchange(jnp.broadcast_to(both, (depth,) + both.shape), "col", quarters)
+    lp, x1, x2 = own_rows(xs, own, own_other, *target_terms(own, own_other))
     away, lp = lax.optimization_barrier((away, lp))
     away_other = swap(away)
     lp = more_rows(x1, x2, away, lp, 1).reshape(lp.shape)

time: 77.3 us -> 76.6 us (level)
  starting transfers between devices: 22.6 us -> 23.9 us
  blocking collectives: 21.3 us -> 20.2 us
    ppermute x3, starting transfers between devices: 3.68 us -> 4.89 us  [along(): return lax.ppermute(values, 'row', pairs)]
    all_to_all x2, blocking collectives: 21.3 us -> 20.2 us  [exchange(): lax.all_to_all(values, axis, 0, 0, tiled=True, axis_index_groups=groups)]
where the time goes in v4:
time: 76.6 us; the launch traced here: 76.2 us
  starting transfers between devices  23.9 us (31%)
  Pallas kernels  23.1 us (30%)
  blocking collectives  20.2 us (26%)
  waiting for transfers between devices  5.84 us (8%)
  local copies, waits for them, and re-layouts  2.34 us (3%)
    all_to_all x2, blocking collectives, exchange(): lax.all_to_all(values, axis, 0, 0, tiled=True, axis_index_groups=groups)  20.2 us
    all_to_all x1, starting transfers between devices, exchange(): lax.all_to_all(values, axis, 0, 0, tiled=True, axis_index_groups=groups)  8.19 us
    ppermute x2, starting transfers between devices, swap(): return lax.ppermute(values, 'row', [(i, i ^ 1) for i in range(rows)])  6.06 us
    pallas_call x2, Pallas kernels, more_rows(): pl.pallas_call(more_kernel, out_shape=jax.ShapeDtypeStruct((copies, rows...  5.89 us
    pallas_call x1, Pallas kernels, first_columns(): pl.pallas_call(first_kernel, out_shape=(jax.ShapeDtypeStruct((count, 2, P...  5.53 us
    pallas_call x1, Pallas kernels, own_rows(): pl.pallas_call(own_kernel, out_shape=(jax.ShapeDtypeStruct((rows // LANES...  5.26 us
    all_to_all x1, waiting for transfers between devices, exchange(): lax.all_to_all(values, axis, 0, 0, tiled=True, axis_index_groups=groups)  5.06 us
    ppermute x3, starting transfers between devices, along(): return lax.ppermute(values, 'row', pairs)  4.89 us
  transfers between devices with their start and end apart: 9, of which 2 were waited for; matrix products, arithmetic and copies ran while one was open for 1% of the time, Pallas kernels for 18%

profile of v4, /device:TPU:1, one launch (start us, length us, event | category | flops | bytes accessed | tf_op | source)
XLA Modules:
  0.0 76.2 jit_solution(16123271574633881432)
XLA Ops:
  0.6 3.8 %collective-permute-start = (bf16[64,128]{1,0:T(8,128)(2,1)}, bf16[64,128]{1,0:T(8,128)(2,1)S(1)}, u32[]{:S(2)}, u32[]{:S(2)}) collective-permute-start(bf16[64,128]{1,0:T(8,128)(2,1)} %bitcast.20), channel_id=1, source_target_pairs={{0,16},{1,17},{2,18},{3,19},{4,20},{5,21},{6,22},{7,23},{8,24},{9,... | collective-permute-start | bytes 49160 | tf_op jit(solution)/shard_map/ppermute | solution.py:395
  4.5 0.8 %copy-done = bf16[512,64]{0,1:T(8,128)(2,1)S(1)} copy-done((bf16[512,64]{0,1:T(8,128)(2,1)S(1)}, bf16[512,64]{0,1:T(8,128)(2,1)}, u32[]{:S(2)}) %copy-start) | copy-done | bytes 65560
  5.3 0.7 copy-done.1
  6.0 0.2 prepare.1
  6.2 1.3 %collective-permute-start.1 = (bf16[272,128]{1,0:T(8,128)(2,1)S(1)}, bf16[272,128]{1,0:T(8,128)(2,1)S(1)}, u32[]{:S(2)}, u32[]{:S(2)}) collective-permute-start(bf16[272,128]{1,0:T(8,128)(2,1)S(1)} %get-tuple-element.22), channel_id=1, source_target_pairs={{0,64},{32,96},{64,128},{96,160},{128,192},{160,224},{192,0},{224,... | collective-permute-start | bytes 208904 | tf_op jit(solution)/shard_map/ppermute | solution.py:387
  7.5 2.5 %collective-permute-start.2 = (bf16[272,128]{1,0:T(8,128)(2,1)S(1)}, bf16[272,128]{1,0:T(8,128)(2,1)S(1)}, u32[]{:S(2)}, u32[]{:S(2)}) collective-permute-start(bf16[272,128]{1,0:T(8,128)(2,1)S(1)} %get-tuple-element.22), channel_id=1, source_target_pairs={{0,128},{32,160},{64,192},{96,224},{128,0},{160,32},{192,64},{224,... | collective-permute-start | bytes 208904 | tf_op jit(solution)/shard_map/ppermute | solution.py:387
  9.9 1.2 %collective-permute-start.3 = (bf16[272,128]{1,0:T(8,128)(2,1)S(1)}, bf16[272,128]{1,0:T(8,128)(2,1)S(1)}, u32[]{:S(2)}, u32[]{:S(2)}) collective-permute-start(bf16[272,128]{1,0:T(8,128)(2,1)S(1)} %get-tuple-element.22), channel_id=1, source_target_pairs={{0,192},{32,224},{64,0},{96,32},{128,64},{160,96},{192,128},{224,1... | collective-permute-start | bytes 208904 | tf_op jit(solution)/shard_map/ppermute | solution.py:387
  11.1 0.0 collective-permute-done
  11.1 0.8 broadcast_in_dim.3
  11.9 8.2 %all-to-all-start = ((bf16[8,2,64,128]{3,2,1,0:T(8,128)(2,1)}), bf16[8,2,64,128]{3,2,1,0:T(8,128)(2,1)S(1)}, u32[]{:S(2)}, u32[]{:S(2)}) async-start(bf16[8,2,64,128]{3,2,1,0:T(8,128)(2,1)} %broadcast_in_dim.3), calls=%async_computation | async-start | bytes 524288 | tf_op jit(solution)/shard_map/all_to_all | solution.py:372
  20.1 0.0 collective-permute-done.1
  20.1 0.0 collective-permute-done.2
  20.1 0.0 collective-permute-done.3
  20.1 2.2 %collective-permute-start.4 = (bf16[4,272,128]{2,1,0:T(8,128)(2,1)S(1)}, bf16[4,272,128]{2,1,0:T(8,128)(2,1)S(1)}, u32[]{:S(2)}, u32[]{:S(2)}) collective-permute-start(bf16[4,272,128]{2,1,0:T(8,128)(2,1)S(1)} %pad_maximum_fusion.y_ref.same), channel_id=1, source_target_pairs={{0,32},{32,0},{64,96},{96,64},{128,160},{160,128},{192,224},{224,1... | collective-permute-start | bytes 835592 | tf_op jit(solution)/shard_map/ppermute | solution.py:390
  22.3 0.4 collective-permute-start.5
  22.7 0.8 %collective-permute-done.4.other_ref.other = bf16[4,272,128]{2,1,0:T(8,128)(2,1)S(1)} collective-permute-done((bf16[4,272,128]{2,1,0:T(8,128)(2,1)S(1)}, bf16[4,272,128]{2,1,0:T(8,128)(2,1)S(1)}, u32[]{:S(2)}, u32[]{:S(2)}) %collective-permute-start.4) | collective-permute-done | bytes 278560 | tf_op jit(solution)/shard_map/ppermute | solution.py:390
  23.5 0.7 target_terms.1
  24.2 5.1 %all-to-all-done.xs_ref = bf16[8,2,64,128]{3,2,1,0:T(8,128)(2,1)S(1)} async-done(((bf16[8,2,64,128]{3,2,1,0:T(8,128)(2,1)}), bf16[8,2,64,128]{3,2,1,0:T(8,128)(2,1)S(1)}, u32[]{:S(2)}, u32[]{:S(2)}) %all-to-all-start) | async-done | bytes 262176 | tf_op jit(solution)/shard_map/all_to_all | solution.py:372
  29.3 5.3 %own_rows.1 = (f32[16,128]{1,0:T(8,128)S(1)}, bf16[2048,128]{1,0:T(8,128)(2,1)S(1)}, bf16[2048,128]{1,0:T(8,128)(2,1)S(1)}) custom-call(bf16[8,2,64,128]{3,2,1,0:T(8,128)(2,1)S(1)} %all-to-all-done.xs_ref, bf16[4,272,128]{2,1,0:T(8,128)(2,1)S(1)} %pad_maximum_fusion.y_ref.same, bf16[4,272,128]{2,1,0:T(8,128)(2,1)S(1)} %collective-permute-done.4.other_ref.other, ...), custom_call_target="tpu_custom_call" | custom-call | flops 2147483648 | bytes 1048576 | tf_op jit(solution)/shard_map/own_rows/pallas_call | solution.py:192
  34.5 0.0 collective-permute-done.5.y_ref.same
  34.5 3.9 %collective-permute-start.6 = (bf16[4,272,128]{2,1,0:T(8,128)(2,1)S(1)}, bf16[4,272,128]{2,1,0:T(8,128)(2,1)S(1)}, u32[]{:S(2)}, u32[]{:S(2)}) collective-permute-start(bf16[4,272,128]{2,1,0:T(8,128)(2,1)S(1)} %collective-permute-done.5.y_ref.same), channel_id=1, source_target_pairs={{0,32},{32,0},{64,96},{96,64},{128,160},{160,128},{192,224},{224,1... | collective-permute-start | bytes 835592 | tf_op jit(solution)/shard_map/ppermute | solution.py:390
  38.4 2.9 %more_rows.2 = f32[1,16,128]{2,1,0:T(8,128)S(1)} custom-call(bf16[2048,128]{1,0:T(8,128)(2,1)S(1)} %get-tuple-element.26.x1, bf16[2048,128]{1,0:T(8,128)(2,1)S(1)} %get-tuple-element.27.x2, bf16[4,272,128]{2,1,0:T(8,128)(2,1)S(1)} %collective-permute-done.5.y_ref.same, f32[16,128]{1,0:T(8,128)S(1)} %get-tuple-element.30.first_ref), custom_call_target="tpu_custom_call" | custom-call | flops 1073741824 | bytes 1048576 | tf_op jit(solution)/shard_map/more_rows/pallas_call | solution.py:207
  41.4 0.0 collective-permute-done.6.y_ref.other
  41.4 3.0 %more_rows.3 = f32[16,16,128]{2,1,0:T(8,128)S(1)} custom-call(bf16[2048,128]{1,0:T(8,128)(2,1)S(1)} %get-tuple-element.26.x1, bf16[2048,128]{1,0:T(8,128)(2,1)S(1)} %get-tuple-element.27.x2, bf16[4,272,128]{2,1,0:T(8,128)(2,1)S(1)} %collective-permute-done.6.y_ref.other, f32[16,128]{1,0:T(8,128)S(1)} %bitcast.26), custom_call_target="tpu_custom_call" | custom-call | flops 1073741824 | bytes 1048576 | tf_op jit(solution)/shard_map/more_rows/pallas_call | solution.py:207
  44.3 0.0 copy-start.3
  44.4 11.6 %all_to_all.15.lp_ref = f32[16,16,128]{2,1,0:T(8,128)S(1)} all-to-all(f32[16,16,128]{2,1,0:T(8,128)S(1)} %more_rows.3), channel_id=1, replica_groups={{0,1,2,3,4,5,6,7,16,17,18,19,20,21,22,23},{8,9,10,11,12,13,14,15,24,25,..., dimensions={0} | all-to-all | bytes 262144 | tf_op jit(solution)/shard_map/all_to_all | solution.py:372
  56.0 5.5 %first_columns.1 = (f32[8,2,256]{2,1,0:T(2,128)S(1)}, f32[16,128]{1,0:T(8,128)S(1)}, f32[2048,128]{1,0:T(8,128)S(1)}, f32[1,128]{1,0:T(1,128)S(1)}) custom-call(bf16[2048,128]{1,0:T(8,128)(2,1)S(1)} %get-tuple-element.26.x1, bf16[2048,128]{1,0:T(8,128)(2,1)S(1)} %get-tuple-element.27.x2, f32[16,16,128]{2,1,0:T(8,128)S(1)} %all_to_all.15.lp_ref, ...), custom_call_target="tpu_custom_call" | custom-call | flops 2147483648 | bytes 4194304 | tf_op jit(solution)/shard_map/first_columns/pallas_call | solution.py:325
  61.5 0.5 collective-permute-start.7
  62.0 4.9 %second_columns.1 = (f32[8,2,256]{2,1,0:T(2,128)S(1)}, f32[1,128]{1,0:T(1,128)S(1)}, f32[4,128]{1,0:T(4,128)S(1)}) custom-call(bf16[2048,128]{1,0:T(8,128)(2,1)S(1)} %get-tuple-element.26.x1, bf16[2048,128]{1,0:T(8,128)(2,1)S(1)} %get-tuple-element.27.x2, f32[2048,128]{1,0:T(8,128)S(1)} %get-tuple-element.31.rows_ref, ...), custom_call_target="tpu_custom_call" | custom-call | flops 2147483648 | bytes 4194304 | tf_op jit(solution)/shard_map/second_columns/pallas_call | solution.py:341
  66.9 0.0 collective-permute-done.7
  66.9 8.6 %all_to_all.16 = f32[8,2,256]{2,1,0:T(2,128)S(1)} all-to-all(f32[8,2,256]{2,1,0:T(2,128)S(1)} %bitcast.30), channel_id=1, replica_groups=mesh['row'=8,'col'=32] {'row'}, dimensions={0} | all-to-all | bytes 32768 | tf_op jit(solution)/shard_map/all_to_all | solution.py:372
  75.6 0.6 finish.1
  (11 shorter events, 0.1 us)
Async XLA Ops:
  0.6 3.8 %copy-start.2 = (f32[512]{0:T(512)S(1)}, f32[512]{0:T(512)}, u32[]{:S(2)}) copy-start(f32[512]{0:T(512)} %param.9) | copy-start | bytes 6148
  0.6 10.5 %collective-permute-start = (bf16[64,128]{1,0:T(8,128)(2,1)}, bf16[64,128]{1,0:T(8,128)(2,1)S(1)}, u32[]{:S(2)}, u32[]{:S(2)}) collective-permute-start(bf16[64,128]{1,0:T(8,128)(2,1)} %bitcast.20), channel_id=1, source_target_pairs={{0,16},{1,17},{2,18},{3,19},{4,20},{5,21},{6,22},{7,23},{8,24},{9,... | collective-permute-start | bytes 49160 | tf_op jit(solution)/shard_map/ppermute | solution.py:395
  4.5 0.8 %copy-start = (bf16[512,64]{0,1:T(8,128)(2,1)S(1)}, bf16[512,64]{0,1:T(8,128)(2,1)}, u32[]{:S(2)}) copy-start(bf16[512,64]{0,1:T(8,128)(2,1)} %param.6) | copy-start | bytes 196612
  5.3 0.7 copy-start.1
  6.2 13.8 %collective-permute-start.1 = (bf16[272,128]{1,0:T(8,128)(2,1)S(1)}, bf16[272,128]{1,0:T(8,128)(2,1)S(1)}, u32[]{:S(2)}, u32[]{:S(2)}) collective-permute-start(bf16[272,128]{1,0:T(8,128)(2,1)S(1)} %get-tuple-element.22), channel_id=1, source_target_pairs={{0,64},{32,96},{64,128},{96,160},{128,192},{160,224},{192,0},{224,... | collective-permute-start | bytes 208904 | tf_op jit(solution)/shard_map/ppermute | solution.py:387
  7.5 12.6 %collective-permute-start.2 = (bf16[272,128]{1,0:T(8,128)(2,1)S(1)}, bf16[272,128]{1,0:T(8,128)(2,1)S(1)}, u32[]{:S(2)}, u32[]{:S(2)}) collective-permute-start(bf16[272,128]{1,0:T(8,128)(2,1)S(1)} %get-tuple-element.22), channel_id=1, source_target_pairs={{0,128},{32,160},{64,192},{96,224},{128,0},{160,32},{192,64},{224,... | collective-permute-start | bytes 208904 | tf_op jit(solution)/shard_map/ppermute | solution.py:387
  9.9 10.1 %collective-permute-start.3 = (bf16[272,128]{1,0:T(8,128)(2,1)S(1)}, bf16[272,128]{1,0:T(8,128)(2,1)S(1)}, u32[]{:S(2)}, u32[]{:S(2)}) collective-permute-start(bf16[272,128]{1,0:T(8,128)(2,1)S(1)} %get-tuple-element.22), channel_id=1, source_target_pairs={{0,192},{32,224},{64,0},{96,32},{128,64},{160,96},{192,128},{224,1... | collective-permute-start | bytes 208904 | tf_op jit(solution)/shard_map/ppermute | solution.py:387
  11.9 17.4 %all-to-all-start = ((bf16[8,2,64,128]{3,2,1,0:T(8,128)(2,1)}), bf16[8,2,64,128]{3,2,1,0:T(8,128)(2,1)S(1)}, u32[]{:S(2)}, u32[]{:S(2)}) async-start(bf16[8,2,64,128]{3,2,1,0:T(8,128)(2,1)} %broadcast_in_dim.3), calls=%async_computation | async-start | bytes 524288 | tf_op jit(solution)/shard_map/all_to_all | solution.py:372
  20.1 3.3 %collective-permute-start.4 = (bf16[4,272,128]{2,1,0:T(8,128)(2,1)S(1)}, bf16[4,272,128]{2,1,0:T(8,128)(2,1)S(1)}, u32[]{:S(2)}, u32[]{:S(2)}) collective-permute-start(bf16[4,272,128]{2,1,0:T(8,128)(2,1)S(1)} %pad_maximum_fusion.y_ref.same), channel_id=1, source_target_pairs={{0,32},{32,0},{64,96},{96,64},{128,160},{160,128},{192,224},{224,1... | collective-permute-start | bytes 835592 | tf_op jit(solution)/shard_map/ppermute | solution.py:390
  22.3 12.2 %collective-permute-start.5 = (bf16[4,272,128]{2,1,0:T(8,128)(2,1)S(1)}, bf16[4,272,128]{2,1,0:T(8,128)(2,1)S(1)}, u32[]{:S(2)}, u32[]{:S(2)}) collective-permute-start(bf16[4,272,128]{2,1,0:T(8,128)(2,1)S(1)} %pad_maximum_fusion.y_ref.same), channel_id=1, source_target_pairs={{0,8},{1,9},{2,10},{3,11},{4,12},{5,13},{6,14},{7,15},{8,0},{9,1},... | collective-permute-start | bytes 835592 | tf_op jit(solution)/shard_map/ppermute | solution.py:383
  34.5 6.8 %collective-permute-start.6 = (bf16[4,272,128]{2,1,0:T(8,128)(2,1)S(1)}, bf16[4,272,128]{2,1,0:T(8,128)(2,1)S(1)}, u32[]{:S(2)}, u32[]{:S(2)}) collective-permute-start(bf16[4,272,128]{2,1,0:T(8,128)(2,1)S(1)} %collective-permute-done.5.y_ref.same), channel_id=1, source_target_pairs={{0,32},{32,0},{64,96},{96,64},{128,160},{160,128},{192,224},{224,1... | collective-permute-start | bytes 835592 | tf_op jit(solution)/shard_map/ppermute | solution.py:390
  44.3 11.6 %copy-start.3 = (f32[4096]{0:T(1024)S(1)}, f32[4096]{0:T(1024)}, u32[]{:S(2)}) copy-start(f32[4096]{0:T(1024)} %param.7) | copy-start | bytes 49156
  56.0 6.0 %copy-start.4 = (f32[4096]{0:T(1024)S(1)}, f32[4096]{0:T(1024)}, u32[]{:S(2)}) copy-start(f32[4096]{0:T(1024)} %param.8) | copy-start | bytes 49156
  61.5 5.3 %collective-permute-start.7 = (f32[8,2,256]{2,1,0:T(2,128)S(1)}, f32[8,2,256]{2,1,0:T(2,128)S(1)}, u32[]{:S(2)}, u32[]{:S(2)}) collective-permute-start(f32[8,2,256]{2,1,0:T(2,128)S(1)} %get-tuple-element.35), channel_id=1, source_target_pairs={{0,8},{1,9},{2,10},{3,11},{4,12},{5,13},{6,14},{7,15},{8,0},{9,1},... | collective-permute-start | bytes 49160 | tf_op jit(solution)/shard_map/ppermute | solution.py:383

commit v5 on v4

--- a/solution.py
+++ b/solution.py
@@ -97,12 +97,23 @@
     return shift
 
 
-def terms_kernel(y_ref, other_ref, h1, h2, shift_ref):
+def terms_kernel(same, other_ref, log_b_ref, h1, h2, shift_ref, base_ref):
+    y_ref = same
     shift = spread_terms(pieces_of((y_ref, other_ref)), h1, h2)
     shift_ref[...] = jnp.full(shift_ref.shape, shift)
-
-
-def target_terms(ys, other):
+    y = same[0, pl.ds(0, PACKED), :].astype(F32).T
+    log_b = log_b_ref[lax.axis_index("row")]
+    for side in range(2):
+        part = y[64 * side : 64 * (side + 1)]
+        sq = jnp.sum(part * part, axis=0, keepdims=True)
+        for k in range(2):
+            row = 2 * side + k
+            base_ref[pl.ds(row, 1), :] = (
+                log_b[row : row + 1] + 0.5 * sq[:, k * LANES : (k + 1) * LANES]
+            )
+
+
+def target_terms(ys, other, log_b):
     packed = 2 * ys.shape[0] * PACKED
     return pl.pallas_call(
         terms_kernel,
@@ -110,10 +121,11 @@
             jax.ShapeDtypeStruct((packed, LANES), F32),
             jax.ShapeDtypeStruct((packed, LANES), F32),
             jax.ShapeDtypeStruct((1, LANES), F32),
+            jax.ShapeDtypeStruct((4, LANES), F32),
         ),
         name="target_terms",
         compiler_params=params(),
-    )(ys, other)
+    )(ys, other, log_b)
 
 
 def row_sums(x1, x2, y_refs, h1, h2, shift, put):
@@ -292,7 +304,7 @@
 
 
 def second_kernel(
-    x1, x2, rows_ref, shift_ref, r_ref, same, other, log_b_ref, lt_ref, f_ref, base_ref
+    x1, x2, rows_ref, shift_ref, r_ref, same, other, lt_ref, f_ref
 ):
     ys = pieces_of((same, other))
     column_sums(x1, x2, rows_ref, shift_ref[:, :1], ys, owners_of(len(ys)), lt_ref)
@@ -300,16 +312,6 @@
     at = col // (2 * depth) * depth + col % depth
     x = x1[pl.ds(pl.multiple_of(at * LANES, LANES), LANES), :].astype(F32).T
     f_ref[...] = r_ref[pl.ds(at, 1), :] + 0.5 * jnp.sum(x * x, axis=0, keepdims=True)
-    y = same[0, pl.ds(0, PACKED), :].astype(F32).T
-    log_b = log_b_ref[lax.axis_index("row")]
-    for side in range(2):
-        part = y[64 * side : 64 * (side + 1)]
-        sq = jnp.sum(part * part, axis=0, keepdims=True)
-        for k in range(2):
-            row = 2 * side + k
-            base_ref[pl.ds(row, 1), :] = (
-                log_b[row : row + 1] + 0.5 * sq[:, k * LANES : (k + 1) * LANES]
-            )
 
 
 def column_cost(rows, count):
@@ -336,19 +338,18 @@
     )(x1, x2, lps, log_a, same, other)
 
 
-def second_columns(x1, x2, weights, shift, r, same, other, log_b):
+def second_columns(x1, x2, weights, shift, r, same, other):
     rows, count = x1.shape[0], 2 * same.shape[0]
     return pl.pallas_call(
         second_kernel,
         out_shape=(
             jax.ShapeDtypeStruct((count, 2, PACKED), F32),
             jax.ShapeDtypeStruct((1, LANES), F32),
-            jax.ShapeDtypeStruct((4, LANES), F32),
         ),
         name="second_columns",
         compiler_params=params(),
         cost_estimate=column_cost(rows, count),
-    )(x1, x2, weights, shift, r, same, other, log_b)
+    )(x1, x2, weights, shift, r, same, other)
 
 
 def finish_kernel(lt_ref, base_ref, own_ref, g_ref, f_ref):
@@ -396,16 +397,18 @@
     quarters = [list(range(k, k + depth)) for k in range(0, cols, depth)]
     both = jnp.stack([one, far])
     xs = exchange(jnp.broadcast_to(both, (depth,) + both.shape), "col", quarters)
-    lp, x1, x2 = own_rows(xs, own, own_other, *target_terms(own, own_other))
+    log_b = log_b.reshape(rows, 4, LANES)
+    *terms, base = target_terms(own, own_other, log_b)
+    lp, x1, x2 = own_rows(xs, own, own_other, *terms)
     away, lp = lax.optimization_barrier((away, lp))
     away_other = swap(away)
     lp = more_rows(x1, x2, away, lp, 1).reshape(lp.shape)
     lps = more_rows(x1, x2, away_other, lp, half)
     lps = exchange(lps, "col", alike)
-    log_a, log_b = log_a.reshape(4, depth, LANES), log_b.reshape(rows, 4, LANES)
+    log_a = log_a.reshape(4, depth, LANES)
     lt_away, r, weights, shift = first_columns(x1, x2, lps, log_a, away, away_other)
     lt_back = partner(lt_away)
-    lt, f, base = second_columns(x1, x2, weights, shift, r, own, own_other, log_b)
+    lt, f = second_columns(x1, x2, weights, shift, r, own, own_other)
     lt = joined(lt, lt_back)
     lt = exchange(lt, "row").reshape(rows, 4, LANES)
     g, f = finish(lt, base, f)

time: 76.6 us -> 76.9 us (level)
  transfers between devices with their start and end apart: 9 -> 9, of which waited for: 2 -> 2; matrix products, arithmetic and copies ran while one was open for 1% -> 1% of each run, Pallas kernels for 18% -> 19%
where the time goes in v5:
time: 76.9 us; the launch traced here: 76.5 us
  starting transfers between devices  23.9 us (31%)
  Pallas kernels  23.4 us (30%)
  blocking collectives  20.2 us (26%)
  waiting for transfers between devices  5.78 us (8%)
  local copies, waits for them, and re-layouts  2.35 us (3%)
  between operations  0.77 us (1%)
    all_to_all x2, blocking collectives, exchange(): lax.all_to_all(values, axis, 0, 0, tiled=True, axis_index_groups=groups)  20.2 us
    all_to_all x1, starting transfers between devices, exchange(): lax.all_to_all(values, axis, 0, 0, tiled=True, axis_index_groups=groups)  8.19 us
    ppermute x2, starting transfers between devices, swap(): return lax.ppermute(values, 'row', [(i, i ^ 1) for i in range(rows)])  6.06 us
    pallas_call x2, Pallas kernels, more_rows(): pl.pallas_call(more_kernel, out_shape=jax.ShapeDtypeStruct((copies, rows...  6.03 us
    pallas_call x1, Pallas kernels, first_columns(): pl.pallas_call(first_kernel, out_shape=(jax.ShapeDtypeStruct((count, 2, P...  5.59 us
    pallas_call x1, Pallas kernels, own_rows(): pl.pallas_call(own_kernel, out_shape=(jax.ShapeDtypeStruct((rows // LANES...  5.38 us
    all_to_all x1, waiting for transfers between devices, exchange(): lax.all_to_all(values, axis, 0, 0, tiled=True, axis_index_groups=groups)  4.99 us
    ppermute x3, starting transfers between devices, along(): return lax.ppermute(values, 'row', pairs)  4.89 us
  transfers between devices with their start and end apart: 9, of which 2 were waited for; matrix products, arithmetic and copies ran while one was open for 1% of the time, Pallas kernels for 19%

profile of v5, /device:TPU:1, one launch (start us, length us, event | category | flops | bytes accessed | tf_op | source)
XLA Modules:
  0.0 76.5 jit_solution(786638065155560109)
XLA Ops:
  0.6 3.8 %collective-permute-start = (bf16[64,128]{1,0:T(8,128)(2,1)}, bf16[64,128]{1,0:T(8,128)(2,1)S(1)}, u32[]{:S(2)}, u32[]{:S(2)}) collective-permute-start(bf16[64,128]{1,0:T(8,128)(2,1)} %bitcast.21), channel_id=1, source_target_pairs={{0,16},{1,17},{2,18},{3,19},{4,20},{5,21},{6,22},{7,23},{8,24},{9,... | collective-permute-start | bytes 49160 | tf_op jit(solution)/shard_map/ppermute | solution.py:396
  4.5 0.8 %copy-done = bf16[512,64]{0,1:T(8,128)(2,1)S(1)} copy-done((bf16[512,64]{0,1:T(8,128)(2,1)S(1)}, bf16[512,64]{0,1:T(8,128)(2,1)}, u32[]{:S(2)}) %copy-start) | copy-done | bytes 65560
  5.3 0.7 copy-done.2
  6.0 0.2 prepare.1
  6.2 1.3 %collective-permute-start.1 = (bf16[272,128]{1,0:T(8,128)(2,1)S(1)}, bf16[272,128]{1,0:T(8,128)(2,1)S(1)}, u32[]{:S(2)}, u32[]{:S(2)}) collective-permute-start(bf16[272,128]{1,0:T(8,128)(2,1)S(1)} %get-tuple-element.22), channel_id=1, source_target_pairs={{0,64},{32,96},{64,128},{96,160},{128,192},{160,224},{192,0},{224,... | collective-permute-start | bytes 208904 | tf_op jit(solution)/shard_map/ppermute | solution.py:388
  7.5 2.5 %collective-permute-start.2 = (bf16[272,128]{1,0:T(8,128)(2,1)S(1)}, bf16[272,128]{1,0:T(8,128)(2,1)S(1)}, u32[]{:S(2)}, u32[]{:S(2)}) collective-permute-start(bf16[272,128]{1,0:T(8,128)(2,1)S(1)} %get-tuple-element.22), channel_id=1, source_target_pairs={{0,128},{32,160},{64,192},{96,224},{128,0},{160,32},{192,64},{224,... | collective-permute-start | bytes 208904 | tf_op jit(solution)/shard_map/ppermute | solution.py:388
  9.9 1.2 %collective-permute-start.3 = (bf16[272,128]{1,0:T(8,128)(2,1)S(1)}, bf16[272,128]{1,0:T(8,128)(2,1)S(1)}, u32[]{:S(2)}, u32[]{:S(2)}) collective-permute-start(bf16[272,128]{1,0:T(8,128)(2,1)S(1)} %get-tuple-element.22), channel_id=1, source_target_pairs={{0,192},{32,224},{64,0},{96,32},{128,64},{160,96},{192,128},{224,1... | collective-permute-start | bytes 208904 | tf_op jit(solution)/shard_map/ppermute | solution.py:388
  11.1 0.0 collective-permute-done
  11.1 0.8 broadcast_in_dim.3
  11.9 8.2 %all-to-all-start = ((bf16[8,2,64,128]{3,2,1,0:T(8,128)(2,1)}), bf16[8,2,64,128]{3,2,1,0:T(8,128)(2,1)S(1)}, u32[]{:S(2)}, u32[]{:S(2)}) async-start(bf16[8,2,64,128]{3,2,1,0:T(8,128)(2,1)} %broadcast_in_dim.3), calls=%async_computation | async-start | bytes 524288 | tf_op jit(solution)/shard_map/all_to_all | solution.py:373
  20.1 0.0 collective-permute-done.2
  20.1 0.0 collective-permute-done.3
  20.1 0.0 copy-start.1
  20.1 2.2 %collective-permute-start.4 = (bf16[4,272,128]{2,1,0:T(8,128)(2,1)S(1)}, bf16[4,272,128]{2,1,0:T(8,128)(2,1)S(1)}, u32[]{:S(2)}, u32[]{:S(2)}) collective-permute-start(bf16[4,272,128]{2,1,0:T(8,128)(2,1)S(1)} %pad_maximum_fusion.same.y_ref), channel_id=1, source_target_pairs={{0,32},{32,0},{64,96},{96,64},{128,160},{160,128},{192,224},{224,1... | collective-permute-start | bytes 835592 | tf_op jit(solution)/shard_map/ppermute | solution.py:391
  22.3 0.4 collective-permute-start.5
  22.7 0.8 %collective-permute-done.4.other_ref.other = bf16[4,272,128]{2,1,0:T(8,128)(2,1)S(1)} collective-permute-done((bf16[4,272,128]{2,1,0:T(8,128)(2,1)S(1)}, bf16[4,272,128]{2,1,0:T(8,128)(2,1)S(1)}, u32[]{:S(2)}, u32[]{:S(2)}) %collective-permute-start.4) | collective-permute-done | bytes 278560 | tf_op jit(solution)/shard_map/ppermute | solution.py:391
  23.5 0.8 %target_terms.1 = (f32[2048,128]{1,0:T(8,128)S(1)}, f32[2048,128]{1,0:T(8,128)S(1)}, f32[1,128]{1,0:T(1,128)S(1)}, f32[4,128]{1,0:T(4,128)S(1)}) custom-call(bf16[4,272,128]{2,1,0:T(8,128)(2,1)S(1)} %pad_maximum_fusion.same.y_ref, bf16[4,272,128]{2,1,0:T(8,128)(2,1)S(1)} %collective-permute-done.4.other_ref.other, f32[8,4,128]{2,1,0:T(4,128)S(1)} %bitcast.19), custom_call_target="tpu_custom_call" | custom-call | tf_op jit(solution)/shard_map/target_terms/pallas_call | solution.py:118
  24.3 5.0 %all-to-all-done.xs_ref = bf16[8,2,64,128]{3,2,1,0:T(8,128)(2,1)S(1)} async-done(((bf16[8,2,64,128]{3,2,1,0:T(8,128)(2,1)}), bf16[8,2,64,128]{3,2,1,0:T(8,128)(2,1)S(1)}, u32[]{:S(2)}, u32[]{:S(2)}) %all-to-all-start) | async-done | bytes 262176 | tf_op jit(solution)/shard_map/all_to_all | solution.py:373
  29.3 5.4 %own_rows.1 = (f32[16,128]{1,0:T(8,128)S(1)}, bf16[2048,128]{1,0:T(8,128)(2,1)S(1)}, bf16[2048,128]{1,0:T(8,128)(2,1)S(1)}) custom-call(bf16[8,2,64,128]{3,2,1,0:T(8,128)(2,1)S(1)} %all-to-all-done.xs_ref, bf16[4,272,128]{2,1,0:T(8,128)(2,1)S(1)} %pad_maximum_fusion.same.y_ref, bf16[4,272,128]{2,1,0:T(8,128)(2,1)S(1)} %collective-permute-done.4.other_ref.other, ...), custom_call_target="tpu_custom_call" | custom-call | flops 2147483648 | bytes 1048576 | tf_op jit(solution)/shard_map/own_rows/pallas_call | solution.py:204
  34.6 0.0 collective-permute-done.5.y_ref.same
  34.7 3.9 %collective-permute-start.6 = (bf16[4,272,128]{2,1,0:T(8,128)(2,1)S(1)}, bf16[4,272,128]{2,1,0:T(8,128)(2,1)S(1)}, u32[]{:S(2)}, u32[]{:S(2)}) collective-permute-start(bf16[4,272,128]{2,1,0:T(8,128)(2,1)S(1)} %collective-permute-done.5.y_ref.same), channel_id=1, source_target_pairs={{0,32},{32,0},{64,96},{96,64},{128,160},{160,128},{192,224},{224,1... | collective-permute-start | bytes 835592 | tf_op jit(solution)/shard_map/ppermute | solution.py:391
  38.6 3.0 %more_rows.2 = f32[1,16,128]{2,1,0:T(8,128)S(1)} custom-call(bf16[2048,128]{1,0:T(8,128)(2,1)S(1)} %get-tuple-element.26.x1, bf16[2048,128]{1,0:T(8,128)(2,1)S(1)} %get-tuple-element.27.x2, bf16[4,272,128]{2,1,0:T(8,128)(2,1)S(1)} %collective-permute-done.5.y_ref.same, f32[16,128]{1,0:T(8,128)S(1)} %get-tuple-element.30.first_ref), custom_call_target="tpu_custom_call" | custom-call | flops 1073741824 | bytes 1048576 | tf_op jit(solution)/shard_map/more_rows/pallas_call | solution.py:219
  41.6 0.0 collective-permute-done.6.y_ref.other
  41.6 3.0 %more_rows.3 = f32[16,16,128]{2,1,0:T(8,128)S(1)} custom-call(bf16[2048,128]{1,0:T(8,128)(2,1)S(1)} %get-tuple-element.26.x1, bf16[2048,128]{1,0:T(8,128)(2,1)S(1)} %get-tuple-element.27.x2, bf16[4,272,128]{2,1,0:T(8,128)(2,1)S(1)} %collective-permute-done.6.y_ref.other, f32[16,128]{1,0:T(8,128)S(1)} %bitcast.26), custom_call_target="tpu_custom_call" | custom-call | flops 1073741824 | bytes 1048576 | tf_op jit(solution)/shard_map/more_rows/pallas_call | solution.py:219
  44.6 0.0 copy-start.4
  44.6 11.6 %all_to_all.15.lp_ref = f32[16,16,128]{2,1,0:T(8,128)S(1)} all-to-all(f32[16,16,128]{2,1,0:T(8,128)S(1)} %more_rows.3), channel_id=1, replica_groups={{0,1,2,3,4,5,6,7,16,17,18,19,20,21,22,23},{8,9,10,11,12,13,14,15,24,25,..., dimensions={0} | all-to-all | bytes 262144 | tf_op jit(solution)/shard_map/all_to_all | solution.py:373
  56.2 5.6 %first_columns.1 = (f32[8,2,256]{2,1,0:T(2,128)S(1)}, f32[16,128]{1,0:T(8,128)S(1)}, f32[2048,128]{1,0:T(8,128)S(1)}, f32[1,128]{1,0:T(1,128)S(1)}) custom-call(bf16[2048,128]{1,0:T(8,128)(2,1)S(1)} %get-tuple-element.26.x1, bf16[2048,128]{1,0:T(8,128)(2,1)S(1)} %get-tuple-element.27.x2, f32[16,16,128]{2,1,0:T(8,128)S(1)} %all_to_all.15.lp_ref, ...), custom_call_target="tpu_custom_call" | custom-call | flops 2147483648 | bytes 4194304 | tf_op jit(solution)/shard_map/first_columns/pallas_call | solution.py:327
  61.8 0.5 collective-permute-start.7
  62.3 4.9 %second_columns.1 = (f32[8,2,256]{2,1,0:T(2,128)S(1)}, f32[1,128]{1,0:T(1,128)S(1)}) custom-call(bf16[2048,128]{1,0:T(8,128)(2,1)S(1)} %get-tuple-element.26.x1, bf16[2048,128]{1,0:T(8,128)(2,1)S(1)} %get-tuple-element.27.x2, f32[2048,128]{1,0:T(8,128)S(1)} %get-tuple-element.31.rows_ref, f32[1,128]{1,0:T(1,128)S(1)} %get-tuple-element.32.shift_ref, ...), custom_call_target="tpu_custom_call" | custom-call | flops 2147483648 | bytes 4194304 | tf_op jit(solution)/shard_map/second_columns/pallas_call | solution.py:343
  67.2 0.0 collective-permute-done.7
  67.2 8.6 %all_to_all.16 = f32[8,2,256]{2,1,0:T(2,128)S(1)} all-to-all(f32[8,2,256]{2,1,0:T(2,128)S(1)} %bitcast.30), channel_id=1, replica_groups=mesh['row'=8,'col'=32] {'row'}, dimensions={0} | all-to-all | bytes 32768 | tf_op jit(solution)/shard_map/all_to_all | solution.py:373
  75.9 0.6 finish.1
  (11 shorter events, 0.1 us)
Async XLA Ops:
  0.6 3.8 %copy-start.3 = (f32[512]{0:T(512)S(1)}, f32[512]{0:T(512)}, u32[]{:S(2)}) copy-start(f32[512]{0:T(512)} %param.9) | copy-start | bytes 6148
  0.6 10.5 %collective-permute-start = (bf16[64,128]{1,0:T(8,128)(2,1)}, bf16[64,128]{1,0:T(8,128)(2,1)S(1)}, u32[]{:S(2)}, u32[]{:S(2)}) collective-permute-start(bf16[64,128]{1,0:T(8,128)(2,1)} %bitcast.21), channel_id=1, source_target_pairs={{0,16},{1,17},{2,18},{3,19},{4,20},{5,21},{6,22},{7,23},{8,24},{9,... | collective-permute-start | bytes 49160 | tf_op jit(solution)/shard_map/ppermute | solution.py:396
  4.5 0.8 %copy-start = (bf16[512,64]{0,1:T(8,128)(2,1)S(1)}, bf16[512,64]{0,1:T(8,128)(2,1)}, u32[]{:S(2)}) copy-start(bf16[512,64]{0,1:T(8,128)(2,1)} %param.6) | copy-start | bytes 196612
  5.3 0.7 copy-start.2
  6.2 13.8 %collective-permute-start.1 = (bf16[272,128]{1,0:T(8,128)(2,1)S(1)}, bf16[272,128]{1,0:T(8,128)(2,1)S(1)}, u32[]{:S(2)}, u32[]{:S(2)}) collective-permute-start(bf16[272,128]{1,0:T(8,128)(2,1)S(1)} %get-tuple-element.22), channel_id=1, source_target_pairs={{0,64},{32,96},{64,128},{96,160},{128,192},{160,224},{192,0},{224,... | collective-permute-start | bytes 208904 | tf_op jit(solution)/shard_map/ppermute | solution.py:388
  7.5 12.6 %collective-permute-start.2 = (bf16[272,128]{1,0:T(8,128)(2,1)S(1)}, bf16[272,128]{1,0:T(8,128)(2,1)S(1)}, u32[]{:S(2)}, u32[]{:S(2)}) collective-permute-start(bf16[272,128]{1,0:T(8,128)(2,1)S(1)} %get-tuple-element.22), channel_id=1, source_target_pairs={{0,128},{32,160},{64,192},{96,224},{128,0},{160,32},{192,64},{224,... | collective-permute-start | bytes 208904 | tf_op jit(solution)/shard_map/ppermute | solution.py:388
  9.9 10.1 %collective-permute-start.3 = (bf16[272,128]{1,0:T(8,128)(2,1)S(1)}, bf16[272,128]{1,0:T(8,128)(2,1)S(1)}, u32[]{:S(2)}, u32[]{:S(2)}) collective-permute-start(bf16[272,128]{1,0:T(8,128)(2,1)S(1)} %get-tuple-element.22), channel_id=1, source_target_pairs={{0,192},{32,224},{64,0},{96,32},{128,64},{160,96},{192,128},{224,1... | collective-permute-start | bytes 208904 | tf_op jit(solution)/shard_map/ppermute | solution.py:388
  11.9 17.4 %all-to-all-start = ((bf16[8,2,64,128]{3,2,1,0:T(8,128)(2,1)}), bf16[8,2,64,128]{3,2,1,0:T(8,128)(2,1)S(1)}, u32[]{:S(2)}, u32[]{:S(2)}) async-start(bf16[8,2,64,128]{3,2,1,0:T(8,128)(2,1)} %broadcast_in_dim.3), calls=%async_computation | async-start | bytes 524288 | tf_op jit(solution)/shard_map/all_to_all | solution.py:373
  20.1 3.4 %copy-start.1 = (f32[4096]{0:T(1024)S(1)}, f32[4096]{0:T(1024)}, u32[]{:S(2)}) copy-start(f32[4096]{0:T(1024)} %param.8) | copy-start | bytes 49156
  20.1 3.3 %collective-permute-start.4 = (bf16[4,272,128]{2,1,0:T(8,128)(2,1)S(1)}, bf16[4,272,128]{2,1,0:T(8,128)(2,1)S(1)}, u32[]{:S(2)}, u32[]{:S(2)}) collective-permute-start(bf16[4,272,128]{2,1,0:T(8,128)(2,1)S(1)} %pad_maximum_fusion.same.y_ref), channel_id=1, source_target_pairs={{0,32},{32,0},{64,96},{96,64},{128,160},{160,128},{192,224},{224,1... | collective-permute-start | bytes 835592 | tf_op jit(solution)/shard_map/ppermute | solution.py:391
  22.3 12.3 %collective-permute-start.5 = (bf16[4,272,128]{2,1,0:T(8,128)(2,1)S(1)}, bf16[4,272,128]{2,1,0:T(8,128)(2,1)S(1)}, u32[]{:S(2)}, u32[]{:S(2)}) collective-permute-start(bf16[4,272,128]{2,1,0:T(8,128)(2,1)S(1)} %pad_maximum_fusion.same.y_ref), channel_id=1, source_target_pairs={{0,8},{1,9},{2,10},{3,11},{4,12},{5,13},{6,14},{7,15},{8,0},{9,1},... | collective-permute-start | bytes 835592 | tf_op jit(solution)/shard_map/ppermute | solution.py:384
  34.7 6.9 %collective-permute-start.6 = (bf16[4,272,128]{2,1,0:T(8,128)(2,1)S(1)}, bf16[4,272,128]{2,1,0:T(8,128)(2,1)S(1)}, u32[]{:S(2)}, u32[]{:S(2)}) collective-permute-start(bf16[4,272,128]{2,1,0:T(8,128)(2,1)S(1)} %collective-permute-done.5.y_ref.same), channel_id=1, source_target_pairs={{0,32},{32,0},{64,96},{96,64},{128,160},{160,128},{192,224},{224,1... | collective-permute-start | bytes 835592 | tf_op jit(solution)/shard_map/ppermute | solution.py:391
  44.6 11.6 %copy-start.4 = (f32[4096]{0:T(1024)S(1)}, f32[4096]{0:T(1024)}, u32[]{:S(2)}) copy-start(f32[4096]{0:T(1024)} %param.7) | copy-start | bytes 49156
  61.8 5.4 %collective-permute-start.7 = (f32[8,2,256]{2,1,0:T(2,128)S(1)}, f32[8,2,256]{2,1,0:T(2,128)S(1)}, u32[]{:S(2)}, u32[]{:S(2)}) collective-permute-start(f32[8,2,256]{2,1,0:T(2,128)S(1)} %get-tuple-element.35), channel_id=1, source_target_pairs={{0,8},{1,9},{2,10},{3,11},{4,12},{5,13},{6,14},{7,15},{8,0},{9,1},... | collective-permute-start | bytes 49160 | tf_op jit(solution)/shard_map/ppermute | solution.py:384
